TPU v7x, 256 devices: a whole 4x4x8 slice. The times are simulated.
256 devices in a mesh: ctx: 32 (over z_hi, y, core), exp: 8 (over x, z_lo).
Axes of the slice: x: 4, y: 4, z: 8 (z_hi: 4, z_lo: 2; z = z_hi * 2 + z_lo), core: 2. Of those that a mesh axis runs over, the one named last changes fastest.
Arguments:
- query: bfloat16 [4096, 8192], P('ctx', 'exp'), may hold values from -200 to 200
- new_kv: bfloat16 [2, 4096, 512], P(None, 'ctx'), may hold values from -6 to 6
- old_kv: bfloat16 [2, 8192, 512], P(None, 'ctx'), may hold values from -4 to 4
- new_pos: int32 [4096], P('ctx'), may hold values from 0 to 4095, as said below
- o_weight: bfloat16 [8192, 4096], P('exp', 'ctx'), may hold values from -1 to 1
- hidden: bfloat16 [4096, 4096], P(('ctx', 'exp')), may hold values from -1.1953125 to 1.1953125
- norm_gain: float32 [4096], replicated, may hold values from 0.5 to 1.5
- expert_ids: int32 [4096, 8], P('ctx'), may hold values from 0 to 63, all different within a row; in each aligned block of 128 rows (0 to 127, 128 to 255, ...) at most 20 rows name the same one
- gate_weights: float32 [4096, 8], P('ctx'), may hold values from 0.1 to 0.6
- w_in: bfloat16 [32, 8, 4096, 768], P('ctx', 'exp'), may hold values from -0.09375 to 0.09375
- w_out: bfloat16 [32, 8, 384, 4096], P('ctx', 'exp'), may hold values from -0.15625 to 0.15625
Outputs:
- mixed: bfloat16 [4096, 4096], P(('ctx', 'exp'))
Inputs may be any that keep to these rules, and one draw needn't show every extreme that they name: `new_pos`: row block c of 128 rows holds two runs of 64 consecutive positions, run p and run 2 * 32 - 1 - p, p a drawn permutation of the row blocks. `expert_ids`: in the rows of one index of ctx no expert is chosen more than 20 times.
All inputs are finite; a program needn't handle non-finite values.
Results may differ from a plain program's by a relative error of at most 0.034.
Values may be sent and summed in bfloat16 or wider, within the bound.
A program may use at most 192 MiB of HBM per device.

v0:
```python
import jax
import jax.numpy as jnp
from jax import lax
from jax.sharding import PartitionSpec as P

HD = 128
TOPK = 8
SPLIT = 4
FFQ = 384
GROUP = 16


def rms_normed(residual, norm_gain):
    return (
        residual * lax.rsqrt(jnp.mean(residual * residual, 1, keepdims=True) + 1e-06) * norm_gain
    ).astype(jnp.bfloat16)


def per_device(
    query,
    new_kv,
    old_kv,
    new_pos,
    o_weight,
    hidden,
    norm_gain,
    expert_ids,
    gate_weights,
    w_in,
    w_out,
):
    exp_index = lax.axis_index("exp")
    n_exp = lax.axis_size("exp")
    n_ctx = lax.axis_size("ctx")
    rows = query.shape[0]
    heads_here = query.shape[1] // HD
    kv_here = max(1, heads_here // GROUP)
    per_kv = heads_here // kv_here
    kv_first = exp_index * heads_here // GROUP
    new_sel = lax.dynamic_slice_in_dim(new_kv, kv_first * HD, kv_here * HD, 2)
    old_sel = lax.dynamic_slice_in_dim(old_kv, kv_first * HD, kv_here * HD, 2)
    queries = query.reshape(rows, kv_here, per_kv, HD)
    scale = 1.0 / HD**0.5
    pos_row = new_pos.reshape(1, rows)
    old_piece = lax.all_gather(old_sel, "ctx", axis=1, tiled=True)
    new_piece = lax.all_gather(new_sel, "ctx", axis=1, tiled=True)
    pos_piece = lax.all_gather(pos_row, "ctx", axis=1, tiled=True)
    keys = jnp.concatenate([old_piece[0], new_piece[0]], 0).reshape(-1, kv_here, HD)
    values = jnp.concatenate([old_piece[1], new_piece[1]], 0).reshape(-1, kv_here, HD)
    allowed = jnp.concatenate(
        [jnp.ones((rows, old_piece.shape[1]), bool), pos_piece[0][None, :] <= new_pos[:, None]], 1
    )
    mask_full = allowed[:, None, None, :]
    scores = jnp.einsum("qkgd,nkd->qkgn", queries, keys, preferred_element_type=jnp.float32) * scale
    scores = jnp.where(mask_full, scores, -1e30)
    top_old = jnp.full((rows, kv_here, per_kv), -1e30, jnp.float32)
    top_new = jnp.maximum(top_old, jnp.max(scores, -1))
    weights = jnp.where(mask_full, jnp.exp(scores - top_new[..., None]), 0.0)
    total_new = jnp.sum(weights, -1)
    acc_new = jnp.einsum(
        "qkgn,nkd->qkgd", weights.astype(jnp.bfloat16), values, preferred_element_type=jnp.float32
    )
    attended = (acc_new / total_new[..., None]).reshape(rows, heads_here * HD).astype(jnp.bfloat16)
    projected = jnp.dot(
        attended,
        lax.all_gather(o_weight, "ctx", axis=1, tiled=True),
        preferred_element_type=jnp.float32,
    )
    own_rows = rows // n_exp
    own_part = lax.dynamic_slice_in_dim(
        projected, exp_index * own_rows, own_rows, 0
    ) + hidden.astype(jnp.float32)
    term = lax.dynamic_update_slice_in_dim(projected, own_part, exp_index * own_rows, 0)
    residual_all = lax.psum(term.astype(jnp.bfloat16), "exp").astype(jnp.float32)
    normed_all = rms_normed(residual_all, norm_gain)
    residual_own = lax.dynamic_slice_in_dim(residual_all, exp_index * own_rows, own_rows, 0)
    exp_local = n_ctx // SPLIT
    experts_all = exp_local * n_exp
    capacity = min(rows, max(2, rows * TOPK // experts_all * 5 // 4))
    pairs = rows * TOPK
    local_ids = (expert_ids - exp_index * exp_local).reshape(pairs)
    inside = (local_ids >= 0) & (local_ids < exp_local)
    onehot = (local_ids[:, None] == jnp.arange(exp_local, dtype=jnp.int32)[None, :]).astype(
        jnp.int32
    )
    ranks = jnp.cumsum(onehot, 0) - onehot
    slot = jnp.sum(ranks * onehot, 1)
    target = jnp.where(inside, local_ids, exp_local)
    token = jnp.arange(pairs, dtype=jnp.int32) // TOPK
    table = jnp.zeros((exp_local, capacity), jnp.int32).at[target, slot].set(token, mode="drop")
    weight_table = (
        jnp.zeros((exp_local, capacity), jnp.float32)
        .at[target, slot]
        .set(gate_weights.reshape(pairs), mode="drop")
    )
    sent = jnp.repeat(normed_all[table], SPLIT, axis=0)
    w_both = w_in[0, 0]
    w_down = w_out[0, 0]
    received = lax.all_to_all(sent, "ctx", split_axis=0, concat_axis=0, tiled=True)
    count = received.shape[1]
    flat = received.reshape(-1, received.shape[2])
    both = jnp.dot(flat, w_both, preferred_element_type=jnp.float32)
    act = (jax.nn.silu(both[:, :FFQ]) * both[:, FFQ:]).astype(jnp.bfloat16)
    part = jnp.dot(act, w_down, preferred_element_type=jnp.float32).astype(jnp.bfloat16)
    returned = lax.all_to_all(
        part.reshape(n_ctx, count, -1), "ctx", split_axis=0, concat_axis=0, tiled=True
    )
    expert_out = jnp.sum(returned.reshape(exp_local, SPLIT, capacity, -1).astype(jnp.float32), 1)
    weighted = expert_out * weight_table[..., None]
    moe_part = (
        jnp.zeros((rows, normed_all.shape[1]), jnp.float32)
        .at[table.reshape(-1)]
        .add(weighted.reshape(exp_local * capacity, -1))
    )
    moe_own = lax.psum_scatter(
        moe_part.astype(jnp.bfloat16), "exp", scatter_dimension=0, tiled=True
    ).astype(jnp.float32)
    return (residual_own + moe_own).astype(jnp.bfloat16)


def solution(mesh):
    return jax.shard_map(
        per_device,
        mesh=mesh,
        in_specs=(
            P("ctx", "exp"),
            P(None, "ctx", None),
            P(None, "ctx", None),
            P("ctx"),
            P("exp", "ctx"),
            P(("ctx", "exp"), None),
            P(),
            P("ctx", None),
            P("ctx", None),
            P("ctx", "exp", None, None),
            P("ctx", "exp", None, None),
        ),
        out_specs=P(("ctx", "exp"), None),
        check_vma=False,
    )
```

profile of v0, /device:TPU:1, one launch (start us, length us, event | category | flops | bytes accessed | tf_op | source)
XLA Modules:
  0.0 705.6 jit_solution(10188782386263807851)
XLA Ops:
  11.6 2.3 reduce-window.6
  14.3 49.0 %all-gather.1 = s32[32,1,128]{2,1,0:T(1,128)S(1)} all-gather(s32[1,1,128]{2,1,0:T(1,128)} %bitcast.113), channel_id=2, replica_groups=mesh['ctx'=32,'exp'=8] {'ctx'}, dimensions={0}, use_global_device_ids=true | all-gather | bytes 16896 | tf_op jit(solution)/shard_map/all_gather | solution.py:47
  63.3 2.5 broadcast_compare_fusion
  65.8 6.6 concatenate.14
  72.5 3.1 slice_bitcast_fusion.3
  75.7 53.5 %all-gather.6.cloned.1.call-done = bf16[2,8192,128]{2,1,0:T(8,128)(2,1)} async-done(((bf16[2,256,128]{2,1,0:T(8,128)(2,1)}), bf16[2,8192,128]{2,1,0:T(8,128)(2,1)}) %all-gather.6.cloned.1.call-update) | async-done | bytes 4194320 | tf_op jit(solution)/shard_map/all_gather | solution.py:45
  129.2 4.0 slice_bitcast_fusion.1
  133.2 21.7 %fusion = (f32[128,8]{0,1:T(8,128)S(1)}, f32[12288,128,8]{1,0,2:T(8,128)}) fusion(pred[128,12288]{0,1:T(8,128)(4,1)S(1)} %copy-done.1, bf16[4096,128]{1,0:T(8,128)(2,1)S(1)} %copy-done.2, bf16[8192,128]{1,0:T(8,128)(2,1)S(1)} %get-tuple-element.6, bf16[128,1024]{1,0:T(8,128)(2,1)S(1)} %copy-done.8), kind=kOutput, calls=%fused_computation.6 | convolution fusion | flops 3265264640 | bytes 55316480 | tf_op jit(solution)/shard_map/qkgd,nkd->qkgn/dot_general | solution.py:54
  154.9 21.8 %fusion.1 = f32[128,8]{0,1:T(8,128)S(1)} fusion(f32[12288,128,8]{1,0,2:T(8,128)} %get-tuple-element.10, f32[128,8]{0,1:T(8,128)S(1)} %broadcast_maximum_fusion, pred[128,12288]{0,1:T(8,128)(4,1)S(1)} %copy-done.1), kind=kLoop, calls=%fused_computation.7 | loop fusion | flops 62913536 | bytes 51912704 | tf_op jit(solution)/shard_map/reduce_sum | solution.py:59
  176.7 22.1 %fusion.24 = bf16[1,128,128,8]{2,1,3,0:T(8,128)(2,1)S(1)} fusion(f32[12288,128,8]{1,0,2:T(8,128)} %get-tuple-element.10, f32[128,8]{0,1:T(8,128)S(1)} %broadcast_maximum_fusion, pred[128,12288]{0,1:T(8,128)(4,1)S(1)} %copy-done.1, bf16[4096,128]{1,0:T(8,128)(2,1)} %get-tuple-element.7, bf16[8192,128]{1,0:T(8,128)(2,1)} %get-tuple-element.5, ...), kind=kOutput, calls=%fused_computation.33 | convolution fusion | flops 3290693632 | bytes 55320576 | tf_op jit(solution)/shard_map/qkgn,nkd->qkgd/dot_general | solution.py:60
  198.8 16.0 %all-gather.10.cloned.1.call-done = bf16[1024,4096]{1,0:T(8,128)(2,1)} async-done(((bf16[1024,128]{1,0:T(8,128)(2,1)}), bf16[1024,4096]{1,0:T(8,128)(2,1)}) %all-gather.10.cloned.1.call-update) | async-done | bytes 8388624 | tf_op jit(solution)/shard_map/all_gather | solution.py:66
  214.8 4.7 fusion.50
  221.1 4.3 scatter_custom_fusion.1
  225.6 73.9 %all-reduce.3.cloned.1.call-done = bf16[128,4096]{1,0:T(8,128)(2,1)} async-done(((bf16[128,4096]{1,0:T(8,128)(2,1)}), bf16[128,4096]{1,0:T(8,128)(2,1)}) %all-reduce.3.cloned.1.call-update) | async-done | bytes 1048592 | tf_op jit(solution)/shard_map/psum | solution.py:74
  301.0 2.5 multiply_convert_fusion
  303.6 5.1 gather_fusion
  308.6 2.4 reshape.196
  311.0 2.2 broadcast_in_dim.55
  313.2 154.3 %all_to_all.10 = bf16[32,20,4096]{2,1,0:T(8,128)(2,1)} all-to-all(bf16[32,20,4096]{2,1,0:T(8,128)(2,1)S(1)} %bitcast.107), channel_id=1, replica_groups=mesh['ctx'=32,'exp'=8] {'ctx'}, dimensions={0} | all-to-all | bytes 10485760 | tf_op jit(solution)/shard_map/all_to_all | solution.py:99
  467.5 7.8 %reshape.181 = bf16[640,4096]{1,0:T(8,128)(2,1)} reshape(bf16[32,20,4096]{2,1,0:T(8,128)(2,1)} %all_to_all.10) | data formatting | bytes 10485760 | tf_op jit(solution)/shard_map/reshape | solution.py:101
  475.3 8.0 %fusion.7 = f32[640,768]{1,0:T(8,128)S(1)} fusion(bf16[640,4096]{1,0:T(8,128)(2,1)} %reshape.181, bf16[1,1,4096,768]{3,2,1,0:T(8,128)(2,1)} %param.20), kind=kOutput, calls=%fused_computation.14 | convolution fusion | flops 4026531840 | bytes 13500416 | tf_op jit(solution)/shard_map/dot_general | solution.py:102
  483.3 4.7 convolution_convert_fusion
  488.0 7.6 %reshape.182 = bf16[32,20,4096]{2,1,0:T(8,128)(2,1)} reshape(bf16[640,4096]{1,0:T(8,128)(2,1)} %convolution_convert_fusion) | data formatting | bytes 10485760 | tf_op jit(solution)/shard_map/reshape | solution.py:106
  495.6 5.6 all-to-all-start.1
  501.5 4.3 scatter_custom_fusion.2
  505.8 135.9 %all-to-all-done.1 = bf16[32,20,4096]{2,1,0:T(8,128)(2,1)} async-done(((bf16[32,20,4096]{2,1,0:T(8,128)(2,1)}), bf16[32,20,4096]{2,1,0:T(8,128)(2,1)}, u32[]{:S(2)}, u32[]{:S(2)}) %all-to-all-start.1) | async-done | bytes 5242912 | tf_op jit(solution)/shard_map/all_to_all | solution.py:105
  641.7 6.0 convert_reduce_fusion
  647.7 3.1 reduce_sum.45
  650.8 6.7 scatter_custom_fusion
  657.5 2.7 convert_element_type.66
  660.3 2.8 convert_element_type.58
  663.1 34.2 %reduce-scatter.2.cloned.1.call-done = bf16[16,4096]{1,0:T(8,128)(2,1)} async-done(((bf16[128,4096]{1,0:T(8,128)(2,1)}), bf16[16,4096]{1,0:T(8,128)(2,1)}) %reduce-scatter.2.cloned.1.call-update) | async-done | bytes 131088 | tf_op jit(solution)/shard_map/reduce_scatter | solution.py:115
  (59 shorter events, 10.7 us)
Async XLA Ops:
  6.5 476.8 %copy-start = (bf16[1,1,384,4096]{3,2,1,0:T(8,128)(2,1)S(1)}, bf16[1,1,384,4096]{3,2,1,0:T(8,128)(2,1)}, u32[]{:S(2)}) copy-start(bf16[1,1,384,4096]{3,2,1,0:T(8,128)(2,1)} %param.21) | copy-start | bytes 9437188
  6.5 66.0 %all-gather.8.cloned.1.call-start = ((), (), s32[]{:S(2)}) async-start(), calls=%async_computation.4 | async-start | bytes 2162688 | tf_op jit(solution)/shard_map/all_gather | solution.py:46
  8.2 121.0 %all-gather.6.cloned.1.call-start = ((), (), s32[]{:S(2)}) async-start(), calls=%async_computation.3 | async-start | bytes 4325376 | tf_op jit(solution)/shard_map/all_gather | solution.py:45
  9.8 205.0 %all-gather.10.cloned.1.call-start = ((), (), s32[]{:S(2)}) async-start(), calls=%async_computation.5 | async-start | bytes 8650752 | tf_op jit(solution)/shard_map/all_gather | solution.py:66
  10.6 288.9 %all-reduce.3.cloned.1.call-start = ((), (), s32[]{:S(2)}) async-start(), calls=%async_computation.6 | async-start | bytes 2097152 | tf_op jit(solution)/shard_map/psum | solution.py:74
  75.7 57.5 %copy-start.8 = (bf16[128,1024]{1,0:T(8,128)(2,1)S(1)}, bf16[128,1024]{1,0:T(8,128)(2,1)}, u32[]{:S(2)}) copy-start(bf16[128,1024]{1,0:T(8,128)(2,1)} %param.11) | copy-start | bytes 786436
  129.2 4.0 copy-start.1
  129.2 4.0 copy-start.2
  214.8 4.7 copy-start.3
  219.5 1.4 copy-start.7
  219.5 1.4 copy-start.6
  219.5 81.5 %copy-start.4 = (f32[4096]{0:T(1024)S(1)}, f32[4096]{0:T(1024)}, u32[]{:S(2)}) copy-start(f32[4096]{0:T(1024)} %param.17) | copy-start | bytes 49156
  495.6 5.7 copy-start.5
  495.6 146.1 %all-to-all-start.1 = ((bf16[32,20,4096]{2,1,0:T(8,128)(2,1)}), bf16[32,20,4096]{2,1,0:T(8,128)(2,1)}, u32[]{:S(2)}, u32[]{:S(2)}) async-start(bf16[32,20,4096]{2,1,0:T(8,128)(2,1)} %reshape.182), calls=%async_computation.1 | async-start | bytes 12582912 | tf_op jit(solution)/shard_map/all_to_all | solution.py:105
  501.2 196.1 %reduce-scatter.2.cloned.1.call-start = ((), (), s32[]{:S(2)}) async-start(), calls=%async_computation.7 | async-start | bytes 1179648 | tf_op jit(solution)/shard_map/reduce_scatter | solution.py:115
Sparse Core Ops, SparseCore 0:
  10.0 58.9 all-gather.7
  71.6 57.5 all-gather.5
  131.7 83.0 all-gather.9
  220.9 78.6 all-reduce.2
  660.4 36.8 reduce-scatter.1
where the time goes:
time: 711 us; the launch traced here: 706 us
  waiting for transfers between devices  314 us (44%)
  blocking collectives  203 us (29%)
  matrix products  61.1 us (9%)
  local copies, waits for them, and re-layouts  54.7 us (8%)
  other arithmetic  53 us (7%)
  between operations  13.4 us (2%)
    all_to_all x1, blocking collectives, per_device(): lax.all_to_all(sent, 'ctx', split_axis=0, concat_axis=0, tiled=True)  154 us
    all_to_all x1, waiting for transfers between devices, per_device(): lax.all_to_all(part.reshape(n_ctx, count, -1), 'ctx', split_axis=0, conca...  136 us
    psum x1, waiting for transfers between devices, per_device(): lax.psum(term.astype(jnp.bfloat16), 'exp').astype(jnp.float32)  73.9 us
    all_gather x1, waiting for transfers between devices, per_device(): old_piece = lax.all_gather(old_sel, 'ctx', axis=1, tiled=True)  53.5 us
    all_gather x1, blocking collectives, per_device(): pos_piece = lax.all_gather(pos_row, 'ctx', axis=1, tiled=True)  49 us
    reduce_scatter x1, waiting for transfers between devices, per_device(): lax.psum_scatter(moe_part.astype(jnp.bfloat16), 'exp', scatter_dimension=...  34.2 us
    dot_general x1, matrix products, per_device(): jnp.einsum('qkgn,nkd->qkgd', weights.astype(jnp.bfloat16), values, prefer...  22.1 us
    reduce_sum x1, other arithmetic, per_device(): total_new = jnp.sum(weights, -1)  21.8 us
  transfers between devices with their start and end apart: 6, of which 5 were waited for; matrix products, arithmetic and copies ran while one was open for 14% of the time, Pallas kernels for 0%

commit v1 on v0

v1 whole, which is shorter than its diff:
```python
import functools

import jax
import jax.numpy as jnp
from jax import lax
from jax.experimental import pallas as pl
from jax.experimental.pallas import tpu as pltpu
from jax.sharding import PartitionSpec as P

HD = 128
TOPK = 8
SPLIT = 4
FFQ = 384
GROUP = 16
CAP = 20
MESH = pl.DeviceIdType.MESH
ARRIVE = (1, 2, 6, 3, 7, 4, 5)


def rms_normed(residual, norm_gain):
    return (
        residual * lax.rsqrt(jnp.mean(residual * residual, 1, keepdims=True) + 1e-06) * norm_gain
    ).astype(jnp.bfloat16)


def place():
    ctx = lax.axis_index("ctx")
    return ctx // 8, (ctx // 2) % 4, ctx % 2, lax.axis_index("exp")


def ctx_of(hi, y, core):
    return lax.rem(hi, 4) * 8 + y * 2 + core


def remote(src, dst, send, recv, device):
    return pltpu.make_async_remote_copy(
        src_ref=src, dst_ref=dst, send_sem=send, recv_sem=recv, device_id=device, device_id_type=MESH
    )


def moe_kernel(
    normed,
    residual_own,
    pick,
    pick_rest,
    mix_hi,
    mix_lo,
    w_in,
    w_out,
    out_ref,
    sent,
    got,
    both,
    rest_in,
    act,
    rest_out,
    part,
    from_core,
    to_pair,
    from_pair,
    to_home,
    home,
    mixed,
    from_exp,
    d_send,
    d_recv,
    f_send,
    f_recv,
    c_send,
    c_recv,
    rc_send,
    rc_recv,
    rf_send,
    rf_recv,
    rd_send,
    rd_recv,
    x_send,
    x_recv,
):
    hi, y, core, e = place()
    width = sent.shape[-1]
    sibling = (ctx_of(hi, y, 1 - core), e)
    pair = (ctx_of(hi, y + 1 - 2 * lax.rem(y, 2), core), e)

    def there(i):
        return (ctx_of(hi + i // 2, y if i % 2 == 0 else 3 - y, core), e)

    def back(i):
        return (ctx_of(hi + 4 - i // 2, y if i % 2 == 0 else 3 - y, core), e)

    def other(d):
        return lax.rem(e + d, 8)

    barrier = pltpu.get_barrier_semaphore()
    for i in range(1, 8):
        pl.semaphore_signal(barrier, inc=1, device_id=there(i), device_id_type=MESH)
    pl.semaphore_signal(barrier, inc=1, device_id=sibling, device_id_type=MESH)
    pl.semaphore_signal(barrier, inc=1, device_id=pair, device_id_type=MESH)
    for d in range(1, 8):
        pl.semaphore_signal(
            barrier, inc=1, device_id=(lax.axis_index("ctx"), other(d)), device_id_type=MESH
        )

    for m in range(4):
        rows = jnp.dot(
            pick[...], normed[:, m * width : (m + 1) * width], preferred_element_type=jnp.float32
        )
        sent[:, m] = rows.astype(jnp.bfloat16).reshape(8, 16, width)
    rest = jnp.zeros((128, width), jnp.float32)
    for m in range(4):
        rest += jnp.dot(
            pick_rest[:, m * 128 : (m + 1) * 128],
            normed[:, m * width : (m + 1) * width],
            preferred_element_type=jnp.float32,
        )
    sent[:, 4] = rest.astype(jnp.bfloat16).reshape(8, 16, width)
    got[0] = sent[0]

    pl.semaphore_wait(barrier, 16)

    d_copy = [
        None if i == 0 else remote(sent.at[i], got.at[i], d_send.at[i], d_recv.at[i], there(i))
        for i in range(8)
    ]
    for i in (4, 5, 2, 6, 3, 7, 1):
        d_copy[i].start()
    f_copy = [
        remote(got.at[i], got.at[16 + i], f_send.at[i], f_recv.at[i], pair) for i in range(8)
    ]
    c_copy = [
        remote(got.at[i], got.at[8 + i], c_send.at[i], c_recv.at[i], sibling) for i in range(8)
    ] + [
        remote(got.at[16 + i], got.at[24 + i], c_send.at[8 + i], c_recv.at[8 + i], sibling)
        for i in range(8)
    ]
    order = (0,) + ARRIVE
    for n in range(8):
        i = order[n]
        if i > 0:
            d_copy[i].wait_recv()
        f_copy[i].start()
        c_copy[i].start()
        if n >= 2:
            f_copy[order[n - 2]].wait_recv()
            c_copy[8 + order[n - 2]].start()

    def regroup(m, rows, columns):
        row = lax.broadcasted_iota(jnp.int32, (rows, columns), 0)
        column = lax.broadcasted_iota(jnp.int32, (rows, columns), 1)
        small, large = (row, column) if rows < columns else (column, row)
        return (large == (small // 4) * 16 + m * 4 + small % 4).astype(jnp.bfloat16)

    def experts(base):
        rest_rows = got[base : base + 16, 4].reshape(256, width)
        for m in range(4):
            rest_in[:, m * width : (m + 1) * width] = jnp.dot(
                regroup(m, 64, 256), rest_rows, preferred_element_type=jnp.float32
            ).astype(jnp.bfloat16)

        @pl.loop(0, 3)
        def _(n):
            columns = pl.ds(pl.multiple_of(n * 256, 256), 256)
            total = jnp.zeros((320, 256), jnp.float32)
            for m in range(4):
                rows = jnp.concatenate(
                    [
                        got[base : base + 16, m].reshape(256, width),
                        rest_in[:, m * width : (m + 1) * width],
                    ],
                    0,
                )
                total += jnp.dot(
                    rows,
                    w_in[m * width : (m + 1) * width, columns],
                    preferred_element_type=jnp.float32,
                )
            both[:, columns] = total

        gate = both[:, :FFQ]
        act[...] = (gate / (1.0 + jnp.exp(-gate)) * both[:, FFQ:]).astype(jnp.bfloat16)
        steps = width // 256

        @pl.loop(0, 4 * steps)
        def _(n):
            columns = pl.ds(pl.multiple_of(n * 256, 256), 256)
            inner = pl.ds(pl.multiple_of((n % steps) * 256, 256), 256)
            result = jnp.dot(
                act[...], w_out[:, columns], preferred_element_type=jnp.float32
            ).astype(jnp.bfloat16)
            part[base : base + 16, n // steps, :, inner] = result[:256].reshape(16, 16, 256)
            rest_out[:, columns] = result[256:]

        rest_part = jnp.zeros((256, width), jnp.float32)
        for m in range(4):
            rest_part += jnp.dot(
                regroup(m, 256, 64),
                rest_out[:, m * width : (m + 1) * width],
                preferred_element_type=jnp.float32,
            )
        part[base : base + 16, 4] = rest_part.astype(jnp.bfloat16).reshape(16, 16, width)

    for i in order:
        c_copy[i].wait_recv()
    experts(0)
    rc_copy = [
        remote(part.at[8 + i], from_core.at[i], rc_send.at[i], rc_recv.at[i], sibling)
        for i in range(8)
    ] + [
        remote(part.at[24 + i], from_core.at[8 + i], rc_send.at[8 + i], rc_recv.at[8 + i], sibling)
        for i in range(8)
    ]
    for i in order:
        rc_copy[i].start()
    for n in (6, 7):
        f_copy[order[n]].wait_recv()
        c_copy[8 + order[n]].start()
    for i in order:
        c_copy[8 + i].wait_recv()
    experts(16)
    for i in order:
        rc_copy[8 + i].start()

    rf_copy = [
        remote(to_pair.at[i], from_pair.at[i], rf_send.at[i], rf_recv.at[i], pair)
        for i in range(8)
    ]
    rd_copy = [
        None if i == 0 else remote(to_home.at[i], home.at[i], rd_send.at[i], rd_recv.at[i], back(i))
        for i in range(8)
    ]
    final = (4, 5, 2, 6, 3, 7, 1, 0)
    for i in final:
        rc_copy[8 + i].wait_recv()
        to_pair[i] = (
            part[16 + i].astype(jnp.float32) + from_core[8 + i].astype(jnp.float32)
        ).astype(jnp.bfloat16)
        rf_copy[i].start()
    for i in final:
        rc_copy[i].wait_recv()
        rf_copy[i].wait_recv()
        total = (
            part[i].astype(jnp.float32)
            + from_core[i].astype(jnp.float32)
            + from_pair[i].astype(jnp.float32)
        ).astype(jnp.bfloat16)
        if i == 0:
            home[0] = total
        else:
            to_home[i] = total
            rd_copy[i].start()
    for i in ARRIVE:
        rd_copy[i].wait_recv()

    for m in range(4):
        rows = jnp.concatenate(
            [home[:, m].reshape(128, width), home[:, 4].reshape(128, width)], 0
        )
        mixed[:, m * width : (m + 1) * width] = (
            jnp.dot(mix_hi[m], rows, preferred_element_type=jnp.float32)
            + jnp.dot(mix_lo[m], rows, preferred_element_type=jnp.float32)
        ).astype(jnp.bfloat16)

    x_copy = [None]
    for d in range(1, 8):
        own = pl.ds(pl.multiple_of(other(d) * 16, 16), 16)
        x_copy.append(
            remote(
                mixed.at[own],
                from_exp.at[d],
                x_send.at[d],
                x_recv.at[d],
                (lax.axis_index("ctx"), other(d)),
            )
        )
        x_copy[d].start()
    total = (
        residual_own[...] + mixed[pl.ds(pl.multiple_of(e * 16, 16), 16), :].astype(jnp.float32)
    )
    for d in range(1, 8):
        x_copy[d].wait_recv()
        total += from_exp[d].astype(jnp.float32)
    out_ref[...] = total.astype(jnp.bfloat16)

    for i in range(8):
        if i > 0:
            d_copy[i].wait_send()
            rd_copy[i].wait_send()
            x_copy[i].wait_send()
        f_copy[i].wait_send()
        rf_copy[i].wait_send()
    for i in range(16):
        c_copy[i].wait_send()
        rc_copy[i].wait_send()


def moe(normed, residual_own, pick, pick_rest, mix_hi, mix_lo, w_in, w_out):
    model = normed.shape[1]
    width = model // 4
    block = (5, 16, width)
    half = jnp.bfloat16
    vmem = pl.BlockSpec(memory_space=pltpu.VMEM)
    dma = pltpu.SemaphoreType.DMA
    return pl.pallas_call(
        moe_kernel,
        out_shape=jax.ShapeDtypeStruct(residual_own.shape, half),
        in_specs=[vmem] * 8,
        out_specs=vmem,
        scratch_shapes=[
            pltpu.VMEM((8,) + block, half),
            pltpu.VMEM((32,) + block, half),
            pltpu.VMEM((320, 2 * FFQ), jnp.float32),
            pltpu.VMEM((64, model), half),
            pltpu.VMEM((320, FFQ), half),
            pltpu.VMEM((64, model), half),
            pltpu.VMEM((32,) + block, half),
            pltpu.VMEM((16,) + block, half),
            pltpu.VMEM((8,) + block, half),
            pltpu.VMEM((8,) + block, half),
            pltpu.VMEM((8,) + block, half),
            pltpu.VMEM((8,) + block, half),
            pltpu.VMEM((128, model), half),
            pltpu.VMEM((8, 16, model), half),
            dma((8,)),
            dma((8,)),
            dma((8,)),
            dma((8,)),
            dma((16,)),
            dma((16,)),
            dma((16,)),
            dma((16,)),
            dma((8,)),
            dma((8,)),
            dma((8,)),
            dma((8,)),
            dma((8,)),
            dma((8,)),
        ],
        compiler_params=pltpu.CompilerParams(
            collective_id=1, has_side_effects=True, vmem_limit_bytes=56 * 2**20
        ),
        name="moe",
    )(normed, residual_own, pick, pick_rest, mix_hi, mix_lo, w_in, w_out)


def tables(expert_ids, gate_weights):
    hi, y, core, e = place()
    i = jnp.arange(8, dtype=jnp.int32)
    local = ((hi + i // 2) % 4) * 2 + ((y // 2) + i) % 2
    expert = e * 8 + local
    ids = expert_ids.T
    hits = ids[None, :, :] == expert[:, None, None]
    member = jnp.any(hits, 1)
    gate = jnp.sum(jnp.where(hits, gate_weights.T[None], 0.0), 1)
    before = jnp.arange(128)[:, None] < jnp.arange(128)[None, :]
    rank = jnp.dot(
        member.astype(jnp.bfloat16), before.astype(jnp.bfloat16), preferred_element_type=jnp.float32
    ).astype(jnp.int32)
    slot = jnp.where(member, rank, -1)
    r = jnp.arange(16, dtype=jnp.int32)
    pick = slot[:, None, :] == r[None, :, None]
    m = jnp.arange(4, dtype=jnp.int32)
    rest = (slot[:, None, None, :] == 16 + (r % 4)[None, :, None, None]) & (
        (r // 4)[None, :, None, None] == m[None, None, :, None]
    )
    mix = jnp.where(pick, gate[:, None, :], 0.0).reshape(128, 128).T
    mix_rest = jnp.where(rest, gate[:, None, None, :], 0.0).reshape(128, 4, 128).transpose(1, 2, 0)
    mix = jnp.concatenate([jnp.broadcast_to(mix[None], (4, 128, 128)), mix_rest], 2)
    mix_hi = mix.astype(jnp.bfloat16)
    mix_lo = (mix - mix_hi.astype(jnp.float32)).astype(jnp.bfloat16)
    return (
        pick.reshape(128, 128).astype(jnp.bfloat16),
        rest.reshape(128, 512).astype(jnp.bfloat16),
        mix_hi,
        mix_lo,
    )


def per_device(
    query,
    new_kv,
    old_kv,
    new_pos,
    o_weight,
    hidden,
    norm_gain,
    expert_ids,
    gate_weights,
    w_in,
    w_out,
):
    exp_index = lax.axis_index("exp")
    n_exp = lax.axis_size("exp")
    rows = query.shape[0]
    heads_here = query.shape[1] // HD
    kv_here = max(1, heads_here // GROUP)
    per_kv = heads_here // kv_here
    kv_first = exp_index * heads_here // GROUP
    new_sel = lax.dynamic_slice_in_dim(new_kv, kv_first * HD, kv_here * HD, 2)
    old_sel = lax.dynamic_slice_in_dim(old_kv, kv_first * HD, kv_here * HD, 2)
    queries = query.reshape(rows, kv_here, per_kv, HD)
    scale = 1.0 / HD**0.5
    pos_row = new_pos.reshape(1, rows)
    old_piece = lax.all_gather(old_sel, "ctx", axis=1, tiled=True)
    new_piece = lax.all_gather(new_sel, "ctx", axis=1, tiled=True)
    pos_piece = lax.all_gather(pos_row, "ctx", axis=1, tiled=True)
    keys = jnp.concatenate([old_piece[0], new_piece[0]], 0).reshape(-1, kv_here, HD)
    values = jnp.concatenate([old_piece[1], new_piece[1]], 0).reshape(-1, kv_here, HD)
    allowed = jnp.concatenate(
        [jnp.ones((rows, old_piece.shape[1]), bool), pos_piece[0][None, :] <= new_pos[:, None]], 1
    )
    mask_full = allowed[:, None, None, :]
    scores = jnp.einsum("qkgd,nkd->qkgn", queries, keys, preferred_element_type=jnp.float32) * scale
    scores = jnp.where(mask_full, scores, -1e30)
    top_new = jnp.max(scores, -1)
    weights = jnp.where(mask_full, jnp.exp(scores - top_new[..., None]), 0.0)
    total_new = jnp.sum(weights, -1)
    acc_new = jnp.einsum(
        "qkgn,nkd->qkgd", weights.astype(jnp.bfloat16), values, preferred_element_type=jnp.float32
    )
    attended = (acc_new / total_new[..., None]).reshape(rows, heads_here * HD).astype(jnp.bfloat16)
    projected = jnp.dot(
        attended,
        lax.all_gather(o_weight, "ctx", axis=1, tiled=True),
        preferred_element_type=jnp.float32,
    )
    own_rows = rows // n_exp
    own_part = lax.dynamic_slice_in_dim(
        projected, exp_index * own_rows, own_rows, 0
    ) + hidden.astype(jnp.float32)
    term = lax.dynamic_update_slice_in_dim(projected, own_part, exp_index * own_rows, 0)
    residual_all = lax.psum(term.astype(jnp.bfloat16), "exp").astype(jnp.float32)
    normed_all = rms_normed(residual_all, norm_gain)
    residual_own = lax.dynamic_slice_in_dim(residual_all, exp_index * own_rows, own_rows, 0)
    return moe(
        normed_all, residual_own, *tables(expert_ids, gate_weights), w_in[0, 0], w_out[0, 0]
    )


def solution(mesh):
    return jax.shard_map(
        per_device,
        mesh=mesh,
        in_specs=(
            P("ctx", "exp"),
            P(None, "ctx", None),
            P(None, "ctx", None),
            P("ctx"),
            P("exp", "ctx"),
            P(("ctx", "exp"), None),
            P(),
            P("ctx", None),
            P("ctx", None),
            P("ctx", "exp", None, None),
            P("ctx", "exp", None, None),
        ),
        out_specs=P(("ctx", "exp"), None),
        check_vma=False,
    )
```

time: 711 us -> 440 us (0.62)
  waiting for transfers between devices: 314 us -> 150 us
  blocking collectives: 203 us -> 49.7 us
  Pallas kernels: 0 us -> 124 us
  local copies, waits for them, and re-layouts: 54.7 us -> 18.2 us
  other arithmetic: 53 us -> 34.5 us
  matrix products: 61.1 us -> 48.4 us
    all_to_all x1 -> x0, blocking collectives: 154 us -> none  [per_device(): lax.all_to_all(sent, 'ctx', split_axis=0, concat_axis=0, tiled=True)]
    all_to_all x1 -> x0, waiting for transfers between devices: 136 us -> none  [per_device(): lax.all_to_all(part.reshape(n_ctx, count, -1), 'ctx', split_axis=0, conca...]
    pallas_call x0 -> x1, Pallas kernels: none -> 124 us  [moe(): pl.pallas_call(moe_kernel, out_shape=jax.ShapeDtypeStruct(residual_own.sh...]
    reduce_scatter x1 -> x0, waiting for transfers between devices: 34.2 us -> none  [per_device(): lax.psum_scatter(moe_part.astype(jnp.bfloat16), 'exp', scatter_dimension=...]
    reshape x4 -> x0, local copies, waits for them, and re-layouts: 15.6 us -> none  [the longest x1 7.84 us: per_device(): flat = received.reshape(-1, received.shape[2])]
    dot_general x2 -> x1, matrix products: 12.7 us -> 0.14 us  [tables(): jnp.dot(member.astype(jnp.bfloat16), before.astype(jnp.bfloat16), preferr...]
    gather x2 -> x0, local copies, waits for them, and re-layouts: 7.44 us -> none  [per_device(): sent = jnp.repeat(normed_all[table], SPLIT, axis=0)]
  transfers between devices with their start and end apart: 6 -> 4, of which waited for: 5 -> 4; matrix products, arithmetic and copies ran while one was open for 14% -> 20% of each run, Pallas kernels for 0% -> 0%
where the time goes in v1:
time: 440 us; the launch traced here: 438 us
  waiting for transfers between devices  150 us (34%)
  Pallas kernels  124 us (28%)
  blocking collectives  49.7 us (11%)
  matrix products  48.4 us (11%)
  other arithmetic  34.5 us (8%)
  local copies, waits for them, and re-layouts  18.2 us (4%)
  between operations  13.4 us (3%)
    pallas_call x1, Pallas kernels, moe(): pl.pallas_call(moe_kernel, out_shape=jax.ShapeDtypeStruct(residual_own.sh...  124 us
    psum x1, waiting for transfers between devices, per_device(): lax.psum(term.astype(jnp.bfloat16), 'exp').astype(jnp.float32)  74.7 us
    all_gather x1, waiting for transfers between devices, per_device(): old_piece = lax.all_gather(old_sel, 'ctx', axis=1, tiled=True)  57.5 us
    all_gather x1, blocking collectives, per_device(): pos_piece = lax.all_gather(pos_row, 'ctx', axis=1, tiled=True)  49.7 us
    dot_general x1, matrix products, per_device(): jnp.einsum('qkgn,nkd->qkgd', weights.astype(jnp.bfloat16), values, prefer...  22 us
    reduce_sum x1, other arithmetic, per_device(): total_new = jnp.sum(weights, -1)  21.8 us
    dot_general x1, matrix products, per_device(): jnp.einsum('qkgd,nkd->qkgn', queries, keys, preferred_element_type=jnp.fl...  21.5 us
    all_gather x1, waiting for transfers between devices, per_device(): lax.all_gather(o_weight, 'ctx', axis=1, tiled=True)  16.3 us
  transfers between devices with their start and end apart: 4, of which 4 were waited for; matrix products, arithmetic and copies ran while one was open for 20% of the time, Pallas kernels for 0%

profile of v1, /device:TPU:1, one launch (start us, length us, event | category | flops | bytes accessed | tf_op | source)
XLA Modules:
  0.0 438.4 jit_solution(9892043420934274983)
XLA Ops:
  6.5 1.5 constant_dynamic-slice_fusion.1
  8.1 0.7 constant_dynamic-slice_fusion.2
  8.9 0.7 all-gather.10.cloned.1.call-update
  9.7 49.7 %all-gather.1 = s32[32,1,128]{2,1,0:T(1,128)S(1)} all-gather(s32[1,1,128]{2,1,0:T(1,128)} %bitcast.112), channel_id=2, replica_groups=mesh['ctx'=32,'exp'=8] {'ctx'}, dimensions={0}, use_global_device_ids=true | all-gather | bytes 16896 | tf_op jit(solution)/shard_map/all_gather | solution.py:405
  59.4 2.5 broadcast_compare_fusion
  61.9 5.7 %concatenate.13 = pred[128,12288]{0,1:T(8,128)(4,1)S(1)} pad(pred[128,4096]{0,1:T(8,128)(4,1)S(1)} %broadcast_compare_fusion, pred[]{:T(512)} %constant.124.clone.1), padding=0_0x8192_0 | pad | bytes 2097153 | tf_op jit(solution)/shard_map/concatenate | solution.py:408
  67.6 0.8 compare_reduce_fusion
  68.4 0.1 fusion.15
  68.6 0.4 all-gather.8.cloned.1.call-done
  69.0 2.7 slice_bitcast_fusion.3
  71.6 57.5 %all-gather.6.cloned.1.call-done = bf16[2,8192,128]{2,1,0:T(8,128)(2,1)} async-done(((bf16[2,256,128]{2,1,0:T(8,128)(2,1)}), bf16[2,8192,128]{2,1,0:T(8,128)(2,1)}) %all-gather.6.cloned.1.call-update) | async-done | bytes 4194320 | tf_op jit(solution)/shard_map/all_gather | solution.py:403
  129.2 3.9 slice_bitcast_fusion.1
  133.1 21.5 %fusion = (f32[128,8]{0,1:T(8,128)S(1)}, f32[12288,128,8]{1,0,2:T(8,128)}) fusion(pred[128,12288]{0,1:T(8,128)(4,1)S(1)} %concatenate.13, bf16[4096,128]{1,0:T(8,128)(2,1)S(1)} %copy-done.2, bf16[8192,128]{1,0:T(8,128)(2,1)S(1)} %get-tuple-element.6, bf16[128,1024]{1,0:T(8,128)(2,1)S(1)} %copy-done.7), kind=kOutput, calls=%fused_computation.2 | convolution fusion | flops 3265264640 | bytes 55316480 | tf_op jit(solution)/shard_map/qkgd,nkd->qkgn/dot_general | solution.py:412
  154.7 21.8 %fusion.1 = f32[128,8]{0,1:T(8,128)S(1)} fusion(f32[12288,128,8]{1,0,2:T(8,128)} %get-tuple-element.12, f32[128,8]{0,1:T(8,128)S(1)} %get-tuple-element.11, pred[128,12288]{0,1:T(8,128)(4,1)S(1)} %concatenate.13), kind=kLoop, calls=%fused_computation.3 | loop fusion | flops 62913536 | bytes 51912704 | tf_op jit(solution)/shard_map/reduce_sum | solution.py:416
  176.4 22.0 %fusion.19 = bf16[1,128,128,8]{2,1,3,0:T(8,128)(2,1)S(1)} fusion(f32[12288,128,8]{1,0,2:T(8,128)} %get-tuple-element.12, f32[128,8]{0,1:T(8,128)S(1)} %get-tuple-element.11, pred[128,12288]{0,1:T(8,128)(4,1)S(1)} %concatenate.13, bf16[4096,128]{1,0:T(8,128)(2,1)S(1)} %get-tuple-element.7, bf16[8192,128]{1,0:T(8,128)(2,1)} %get-tuple-element.5, ...), kind=kOutput, calls=%fused_computation.23 | convolution fusion | flops 3290693632 | bytes 55320576 | tf_op jit(solution)/shard_map/qkgn,nkd->qkgd/dot_general | solution.py:417
  198.5 16.3 %all-gather.10.cloned.1.call-done = bf16[1024,4096]{1,0:T(8,128)(2,1)} async-done(((bf16[1024,128]{1,0:T(8,128)(2,1)}), bf16[1024,4096]{1,0:T(8,128)(2,1)}) %all-gather.10.cloned.1.call-update) | async-done | bytes 8388624 | tf_op jit(solution)/shard_map/all_gather | solution.py:423
  214.8 4.7 %fusion.42 = f32[128,4096]{1,0:T(8,128)S(1)} fusion(bf16[128,1024]{0,1:T(8,128)(2,1)S(1)} %bitcast.102, bf16[1024,4096]{1,0:T(8,128)(2,1)} %all-gather.10.cloned.1.call-done), kind=kOutput, calls=%fused_computation.78 | convolution fusion | flops 1073741824 | bytes 10747904 | tf_op jit(solution)/shard_map/dot_general | solution.py:421
  219.6 1.2 convert_element_type.51
  221.0 0.1 copy.31
  221.2 0.1 and_convert_fusion
  221.3 0.7 copy.45
  222.0 0.7 bitcast_compare_fusion
  223.1 0.1 copy.30
  223.4 0.7 fusion.23.mix_hi
  224.1 0.7 fusion.24.mix_lo
  224.9 74.7 %all-reduce.3.cloned.1.call-done = bf16[128,4096]{1,0:T(8,128)(2,1)} async-done(((bf16[128,4096]{1,0:T(8,128)(2,1)}), bf16[128,4096]{1,0:T(8,128)(2,1)}) %all-reduce.3.cloned.1.call-update) | async-done | bytes 1048592 | tf_op jit(solution)/shard_map/psum | solution.py:431
  299.6 1.5 multiply_reduce_fusion
  301.1 1.4 convert_element_type.52
  302.5 0.7 constant_dynamic-slice_fusion.residual_own
  303.3 2.6 multiply_convert_fusion.normed
  305.9 124.4 %moe.1 = bf16[16,4096]{1,0:T(8,128)(2,1)} custom-call(bf16[128,4096]{1,0:T(8,128)(2,1)} %multiply_convert_fusion.normed, f32[16,4096]{1,0:T(8,128)} %constant_dynamic-slice_fusion.residual_own, bf16[128,128]{1,0:T(8,128)(2,1)} %get-tuple-element.10.pick, bf16[128,512]{1,0:T(8,128)(2,1)} %bitcast.103, bf16[4,128,256]{2,1,0:T(8,128)(2,1)} %fusion.23.mix_hi, ...), custom_call_target="tpu_custom_call" | custom-call | tf_op jit(solution)/shard_map/moe/pallas_call | solution.py:303
  430.3 1.6 copy.49
  (42 shorter events, 1.1 us)
Async XLA Ops:
  6.5 1.6 copy-start
  6.5 62.4 %all-gather.8.cloned.1.call-start = ((), (), s32[]{:S(2)}) async-start(), calls=%async_computation.1 | async-start | bytes 2162688 | tf_op jit(solution)/shard_map/all_gather | solution.py:404
  8.1 121.1 %all-gather.6.cloned.1.call-start = ((), (), s32[]{:S(2)}) async-start(), calls=%async_computation | async-start | bytes 4325376 | tf_op jit(solution)/shard_map/all_gather | solution.py:403
  8.8 206.0 %all-gather.10.cloned.1.call-start = ((), (), s32[]{:S(2)}) async-start(), calls=%async_computation.2 | async-start | bytes 8650752 | tf_op jit(solution)/shard_map/all_gather | solution.py:423
  9.6 290.0 %all-reduce.3.cloned.1.call-start = ((), (), s32[]{:S(2)}) async-start(), calls=%async_computation.3 | async-start | bytes 2097152 | tf_op jit(solution)/shard_map/psum | solution.py:431
  68.6 64.5 %copy-start.7 = (bf16[128,1024]{1,0:T(8,128)(2,1)S(1)}, bf16[128,1024]{1,0:T(8,128)(2,1)}, u32[]{:S(2)}) copy-start(bf16[128,1024]{1,0:T(8,128)(2,1)} %param.11) | copy-start | bytes 786436
  129.2 3.9 copy-start.2
  214.8 4.7 %copy-start.3 = (bf16[16,4096]{1,0:T(8,128)(2,1)S(1)}, bf16[16,4096]{1,0:T(8,128)(2,1)}, u32[]{:S(2)}) copy-start(bf16[16,4096]{1,0:T(8,128)(2,1)} %param.16) | copy-start | bytes 393220
  214.8 7.9 %copy-start.5 = (s32[128,8]{0,1:T(8,128)S(1)}, s32[128,8]{0,1:T(8,128)}, u32[]{:S(2)}) copy-start(s32[128,8]{0,1:T(8,128)} %param.18) | copy-start | bytes 12292
  214.8 7.9 %copy-start.6 = (f32[128,8]{0,1:T(8,128)S(1)}, f32[128,8]{0,1:T(8,128)}, u32[]{:S(2)}) copy-start(f32[128,8]{0,1:T(8,128)} %param.19) | copy-start | bytes 12292
  219.5 83.7 %copy-start.4 = (f32[4096]{0:T(1024)S(1)}, f32[4096]{0:T(1024)}, u32[]{:S(2)}) copy-start(f32[4096]{0:T(1024)} %param.17) | copy-start | bytes 49156
  303.3 128.6 %copy-start.1 = (bf16[2,256,512]{2,1,0:T(8,128)(2,1)S(1)}, bf16[2,256,512]{2,1,0:T(8,128)(2,1)}, u32[]{:S(2)}) copy-start(bf16[2,256,512]{2,1,0:T(8,128)(2,1)} %param.13) | copy-start | bytes 1572868
Sparse Core Ops, SparseCore 0:
  10.0 58.9 all-gather.7
  71.6 57.5 all-gather.5
  131.7 83.0 all-gather.9
  220.9 78.6 all-reduce.2

commit v2 on v1

--- a/solution.py
+++ b/solution.py
@@ -1,5 +1,3 @@
-import functools
-
 import jax
 import jax.numpy as jnp
 from jax import lax
@@ -8,19 +6,9 @@
 from jax.sharding import PartitionSpec as P
 
 HD = 128
-TOPK = 8
-SPLIT = 4
 FFQ = 384
-GROUP = 16
-CAP = 20
 MESH = pl.DeviceIdType.MESH
 ARRIVE = (1, 2, 6, 3, 7, 4, 5)
-
-
-def rms_normed(residual, norm_gain):
-    return (
-        residual * lax.rsqrt(jnp.mean(residual * residual, 1, keepdims=True) + 1e-06) * norm_gain
-    ).astype(jnp.bfloat16)
 
 
 def place():
@@ -36,6 +24,335 @@
     return pltpu.make_async_remote_copy(
         src_ref=src, dst_ref=dst, send_sem=send, recv_sem=recv, device_id=device, device_id_type=MESH
     )
+
+
+def attention_kernel(
+    query,
+    new_kv,
+    old_kv,
+    new_pos,
+    o_weight,
+    hidden,
+    norm_gain,
+    normed_ref,
+    residual_ref,
+    kv,
+    weight,
+    queries,
+    bias,
+    top,
+    acc,
+    attended,
+    projected,
+    from_exp,
+    own_normed,
+    normed,
+    kz_send,
+    kz_recv,
+    ky_send,
+    ky_recv,
+    kc_send,
+    kc_recv,
+    wz_send,
+    wz_recv,
+    wy_send,
+    wy_recv,
+    wc_send,
+    wc_recv,
+    x_send,
+    x_recv,
+    n_send,
+    n_recv,
+):
+    hi, y, core, e = place()
+    ctx = lax.axis_index("ctx")
+    model = hidden.shape[1]
+    sibling = (ctx_of(hi, y, 1 - core), e)
+    up = (ctx_of(hi, lax.rem(y + 1, 4), core), e)
+    down = (ctx_of(hi, lax.rem(y + 3, 4), core), e)
+
+    def along(d):
+        return (ctx_of(hi + d, y, core), e)
+
+    def other(d):
+        return lax.rem(e + d, 8)
+
+    barrier = pltpu.get_barrier_semaphore()
+    for device in (along(1), along(2), along(3), up, down, sibling):
+        pl.semaphore_signal(barrier, inc=1, device_id=device, device_id_type=MESH)
+    for d in range(1, 8):
+        pl.semaphore_signal(barrier, inc=1, device_id=(ctx, other(d)), device_id_type=MESH)
+
+    lanes = pl.ds(pl.multiple_of((e // 2) * HD, HD), HD)
+    kv[0, 0:256] = old_kv[0, :, lanes]
+    kv[0, 256:384] = new_kv[0, :, lanes]
+    for b in range(3):
+        values = new_kv[1, :, lanes] if b == 2 else old_kv[1, b * 128 : (b + 1) * 128, lanes]
+        kv[0, 384 + b * 128 : 512 + b * 128] = values.astype(jnp.float32).T.astype(jnp.bfloat16)
+    own_pos = new_pos[...]
+    row = lax.broadcasted_iota(jnp.int32, (16, 128), 0)
+    kv[0, 768:784] = (
+        jnp.where(row == 0, own_pos >> 6, jnp.where(row == 1, own_pos & 63, 0))
+        .astype(jnp.float32)
+        .astype(jnp.bfloat16)
+    )
+    weight[0] = o_weight[...]
+
+    pl.semaphore_wait(barrier, 13)
+
+    def gather(blocks, z_send, z_recv, y_send, y_recv, c_send, c_recv):
+        z_copy = [None] + [
+            remote(blocks.at[0], blocks.at[d], z_send.at[d], z_recv.at[d], along(d))
+            for d in range(1, 4)
+        ]
+        y_copy = {}
+        for d in range(4):
+            for dy, device in ((1, up), (3, down)):
+                y_copy[dy, d] = remote(
+                    blocks.at[d],
+                    blocks.at[dy * 4 + d],
+                    y_send.at[dy * 4 + d],
+                    y_recv.at[dy * 4 + d],
+                    device,
+                )
+            source = 4 + d if d % 2 == 0 else 12 + d
+            y_copy[2, d] = remote(
+                blocks.at[source],
+                blocks.at[8 + d],
+                y_send.at[8 + d],
+                y_recv.at[8 + d],
+                up if d % 2 == 0 else down,
+            )
+        c_copy = [
+            remote(blocks.at[s], blocks.at[16 + s], c_send.at[s], c_recv.at[s], sibling)
+            for s in range(16)
+        ]
+        return z_copy, y_copy, c_copy
+
+    kz, ky, kc = gather(kv, kz_send, kz_recv, ky_send, ky_recv, kc_send, kc_recv)
+    wz, wy, wc = gather(weight, wz_send, wz_recv, wy_send, wy_recv, wc_send, wc_recv)
+
+    def begin_y(y_copy, c_copy, d):
+        y_copy[1, d].start()
+        y_copy[3, d].start()
+        c_copy[d].start()
+
+    def pass_on(y_copy, c_copy, d):
+        y_copy[1, d].wait_recv()
+        if d % 2 == 0:
+            y_copy[2, d].start()
+        c_copy[4 + d].start()
+        y_copy[3, d].wait_recv()
+        if d % 2 == 1:
+            y_copy[2, d].start()
+        c_copy[12 + d].start()
+
+    def last(y_copy, c_copy, d):
+        y_copy[2, d].wait_recv()
+        c_copy[8 + d].start()
+
+    near = (0, 1, 3, 2)
+    for d in (1, 3, 2):
+        kz[d].start()
+    begin_y(ky, kc, 0)
+
+    for h in range(8):
+        part = query[:, h * HD : (h + 1) * HD].astype(jnp.float32).T.astype(jnp.bfloat16)
+        queries[h // 2, :, (h % 2) * 128 : (h % 2 + 1) * 128] = part
+    top[...] = jnp.full_like(top, -1e30)
+    acc[...] = jnp.zeros_like(acc)
+    factor = 1.4426950408889634 / HD**0.5
+
+    def attend(group):
+        base = group * 4
+        for b in range(4):
+            digits = kv[base + b, 768:784].astype(jnp.float32)
+            place_of = digits[0:1] * 64.0 + digits[1:2]
+            column = jnp.broadcast_to(place_of, (128, 128)).T
+            seen = column <= own_pos.astype(jnp.float32)
+            bias[b] = jnp.where(seen, 0.0, -1e30)
+
+        @pl.loop(0, 4)
+        def _(t):
+            part = queries[t]
+            pieces = []
+            for b in range(4):
+                scores = jnp.dot(kv[base + b, 0:384], part, preferred_element_type=jnp.float32)
+                wide = jnp.concatenate([bias[b], bias[b]], 1)
+                pieces += [scores[:256], scores[256:] + wide]
+            old_top = top[t, 0:1]
+            new_top = old_top
+            for piece in pieces:
+                new_top = jnp.maximum(new_top, jnp.max(piece, 0, keepdims=True))
+            probs = jnp.concatenate(
+                [jnp.exp2((piece - new_top) * factor).astype(jnp.bfloat16) for piece in pieces], 0
+            )
+            values = jnp.concatenate(
+                [
+                    kv[base + b, 384 + 128 * i : 512 + 128 * i]
+                    for b in range(4)
+                    for i in range(3)
+                ],
+                1,
+            )
+            ones = jnp.ones((16, values.shape[1]), jnp.bfloat16)
+            added = jnp.dot(
+                jnp.concatenate([values, ones], 0), probs, preferred_element_type=jnp.float32
+            )
+            acc[t] = acc[t] * jnp.exp2((old_top - new_top) * factor) + added
+            top[t] = jnp.broadcast_to(new_top, (8, 256))
+
+    for d in (1, 3, 2):
+        kz[d].wait_recv()
+        begin_y(ky, kc, d)
+    for d in (1, 3, 2):
+        wz[d].start()
+    attend(0)
+    for d in near:
+        pass_on(ky, kc, d)
+    begin_y(wy, wc, 0)
+    for d in near:
+        kc[d].wait_recv()
+    attend(4)
+    for d in (1, 3, 2):
+        wz[d].wait_recv()
+        begin_y(wy, wc, d)
+    attend(1)
+    for d in near:
+        last(ky, kc, d)
+    attend(3)
+    for d in near:
+        pass_on(wy, wc, d)
+    attend(2)
+    for d in near:
+        kc[4 + d].wait_recv()
+    attend(5)
+    for d in near:
+        kc[12 + d].wait_recv()
+    attend(7)
+    for d in near:
+        last(wy, wc, d)
+    for d in near:
+        kc[8 + d].wait_recv()
+    attend(6)
+
+    for h in range(8):
+        part = slice((h % 2) * 128, (h % 2 + 1) * 128)
+        scaled = acc[h // 2, 0:128, part] / acc[h // 2, 128:129, part]
+        attended[:, h * HD : (h + 1) * HD] = scaled.T.astype(jnp.bfloat16)
+    for s in range(16):
+        wc[s].wait_recv()
+
+    def column_of(slot):
+        k, dy, dh = slot // 16, (slot // 4) % 4, slot % 4
+        owner = ctx_of(hi + 4 - dh, lax.rem(y + 4 - dy, 4), lax.rem(core + k, 2))
+        return pl.ds(pl.multiple_of(owner * 128, 128), 128)
+
+    @pl.loop(0, 16)
+    def _(n):
+        both = jnp.concatenate([weight[2 * n], weight[2 * n + 1]], 1)
+        result = jnp.dot(attended[...], both, preferred_element_type=jnp.float32)
+        result = result.astype(jnp.bfloat16)
+        projected[:, column_of(2 * n)] = result[:, :128]
+        projected[:, column_of(2 * n + 1)] = result[:, 128:]
+
+    def rows_of(index):
+        return pl.ds(pl.multiple_of(index * 16, 16), 16)
+
+    x_copy = [None] + [
+        remote(
+            projected.at[rows_of(other(d))],
+            from_exp.at[d],
+            x_send.at[d],
+            x_recv.at[d],
+            (ctx, other(d)),
+        )
+        for d in range(1, 8)
+    ]
+    for d in range(1, 8):
+        x_copy[d].start()
+    residual = hidden[...].astype(jnp.float32) + projected[rows_of(e), :].astype(jnp.float32)
+    for d in range(1, 8):
+        x_copy[d].wait_recv()
+        residual += from_exp[d].astype(jnp.float32)
+    residual_ref[...] = residual
+    mean = jnp.sum(residual * residual, 1, keepdims=True) * (1.0 / model)
+    own = (residual * lax.rsqrt(mean + 1e-06) * norm_gain[...]).astype(jnp.bfloat16)
+    own_normed[...] = own
+    n_copy = [None] + [
+        remote(own_normed, normed.at[rows_of(e)], n_send.at[d], n_recv.at[d], (ctx, other(d)))
+        for d in range(1, 8)
+    ]
+    for d in range(1, 8):
+        n_copy[d].start()
+    normed[rows_of(e), :] = own
+    for d in range(1, 8):
+        n_copy[d].wait_recv()
+    normed_ref[...] = normed[...]
+
+    for d in range(1, 4):
+        kz[d].wait_send()
+        wz[d].wait_send()
+    for d in range(4):
+        for dy in range(1, 4):
+            ky[dy, d].wait_send()
+            wy[dy, d].wait_send()
+    for s in range(16):
+        kc[s].wait_send()
+        wc[s].wait_send()
+    for d in range(1, 8):
+        x_copy[d].wait_send()
+        n_copy[d].wait_send()
+
+
+def attention(query, new_kv, old_kv, new_pos, o_weight, hidden, norm_gain):
+    rows = query.shape[0]
+    model = hidden.shape[1]
+    half = jnp.bfloat16
+    vmem = pl.BlockSpec(memory_space=pltpu.VMEM)
+    dma = pltpu.SemaphoreType.DMA
+    return pl.pallas_call(
+        attention_kernel,
+        out_shape=(
+            jax.ShapeDtypeStruct((rows, model), half),
+            jax.ShapeDtypeStruct(hidden.shape, jnp.float32),
+        ),
+        in_specs=[vmem] * 7,
+        out_specs=(vmem, vmem),
+        scratch_shapes=[
+            pltpu.VMEM((32, 784, HD), half),
+            pltpu.VMEM((32,) + o_weight.shape, half),
+            pltpu.VMEM((4, HD, 256), half),
+            pltpu.VMEM((4, 128, 128), jnp.float32),
+            pltpu.VMEM((4, 8, 256), jnp.float32),
+            pltpu.VMEM((4, 144, 256), jnp.float32),
+            pltpu.VMEM(query.shape, half),
+            pltpu.VMEM((rows, model), half),
+            pltpu.VMEM((8, 16, model), half),
+            pltpu.VMEM((16, model), half),
+            pltpu.VMEM((rows, model), half),
+            dma((4,)),
+            dma((4,)),
+            dma((16,)),
+            dma((16,)),
+            dma((16,)),
+            dma((16,)),
+            dma((4,)),
+            dma((4,)),
+            dma((16,)),
+            dma((16,)),
+            dma((16,)),
+            dma((16,)),
+            dma((8,)),
+            dma((8,)),
+            dma((8,)),
+            dma((8,)),
+        ],
+        compiler_params=pltpu.CompilerParams(
+            collective_id=2, has_side_effects=True, vmem_limit_bytes=56 * 2**20
+        ),
+        name="attention",
+    )(query, new_kv, old_kv, new_pos.reshape(1, rows), o_weight, hidden, norm_gain.reshape(1, model))
 
 
 def moe_kernel(
@@ -388,51 +705,11 @@
     w_in,
     w_out,
 ):
-    exp_index = lax.axis_index("exp")
-    n_exp = lax.axis_size("exp")
-    rows = query.shape[0]
-    heads_here = query.shape[1] // HD
-    kv_here = max(1, heads_here // GROUP)
-    per_kv = heads_here // kv_here
-    kv_first = exp_index * heads_here // GROUP
-    new_sel = lax.dynamic_slice_in_dim(new_kv, kv_first * HD, kv_here * HD, 2)
-    old_sel = lax.dynamic_slice_in_dim(old_kv, kv_first * HD, kv_here * HD, 2)
-    queries = query.reshape(rows, kv_here, per_kv, HD)
-    scale = 1.0 / HD**0.5
-    pos_row = new_pos.reshape(1, rows)
-    old_piece = lax.all_gather(old_sel, "ctx", axis=1, tiled=True)
-    new_piece = lax.all_gather(new_sel, "ctx", axis=1, tiled=True)
-    pos_piece = lax.all_gather(pos_row, "ctx", axis=1, tiled=True)
-    keys = jnp.concatenate([old_piece[0], new_piece[0]], 0).reshape(-1, kv_here, HD)
-    values = jnp.concatenate([old_piece[1], new_piece[1]], 0).reshape(-1, kv_here, HD)
-    allowed = jnp.concatenate(
-        [jnp.ones((rows, old_piece.shape[1]), bool), pos_piece[0][None, :] <= new_pos[:, None]], 1
+    normed, residual_own = attention(
+        query, new_kv, old_kv, new_pos, o_weight, hidden, norm_gain
     )
-    mask_full = allowed[:, None, None, :]
-    scores = jnp.einsum("qkgd,nkd->qkgn", queries, keys, preferred_element_type=jnp.float32) * scale
-    scores = jnp.where(mask_full, scores, -1e30)
-    top_new = jnp.max(scores, -1)
-    weights = jnp.where(mask_full, jnp.exp(scores - top_new[..., None]), 0.0)
-    total_new = jnp.sum(weights, -1)
-    acc_new = jnp.einsum(
-        "qkgn,nkd->qkgd", weights.astype(jnp.bfloat16), values, preferred_element_type=jnp.float32
-    )
-    attended = (acc_new / total_new[..., None]).reshape(rows, heads_here * HD).astype(jnp.bfloat16)
-    projected = jnp.dot(
-        attended,
-        lax.all_gather(o_weight, "ctx", axis=1, tiled=True),
-        preferred_element_type=jnp.float32,
-    )
-    own_rows = rows // n_exp
-    own_part = lax.dynamic_slice_in_dim(
-        projected, exp_index * own_rows, own_rows, 0
-    ) + hidden.astype(jnp.float32)
-    term = lax.dynamic_update_slice_in_dim(projected, own_part, exp_index * own_rows, 0)
-    residual_all = lax.psum(term.astype(jnp.bfloat16), "exp").astype(jnp.float32)
-    normed_all = rms_normed(residual_all, norm_gain)
-    residual_own = lax.dynamic_slice_in_dim(residual_all, exp_index * own_rows, own_rows, 0)
     return moe(
-        normed_all, residual_own, *tables(expert_ids, gate_weights), w_in[0, 0], w_out[0, 0]
+        normed, residual_own, *tables(expert_ids, gate_weights), w_in[0, 0], w_out[0, 0]
     )
 
 

time: 440 us -> 249 us (0.57)
  waiting for transfers between devices: 150 us -> 0 us
  Pallas kernels: 124 us -> 242 us
  blocking collectives: 49.7 us -> 0 us
  matrix products: 48.4 us -> 0.14 us
  other arithmetic: 34.5 us -> 4.2 us
  local copies, waits for them, and re-layouts: 18.2 us -> 2.92 us
  between operations: 13.4 us -> 0.11 us
    pallas_call x0 -> x1, Pallas kernels: none -> 119 us  [attention(): pl.pallas_call(attention_kernel, out_shape=(jax.ShapeDtypeStruct((rows, m...]
    psum x1 -> x0, waiting for transfers between devices: 74.7 us -> none  [per_device(): lax.psum(term.astype(jnp.bfloat16), 'exp').astype(jnp.float32)]
    all_gather x3 -> x0, waiting for transfers between devices: 74.3 us -> none  [the longest x1 57.5 us: per_device(): old_piece = lax.all_gather(old_sel, 'ctx', axis=1, tiled=True)]
    all_gather x1 -> x0, blocking collectives: 49.7 us -> none  [per_device(): pos_piece = lax.all_gather(pos_row, 'ctx', axis=1, tiled=True)]
    dot_general x3 -> x0, matrix products: 48.3 us -> none  [the longest x1 22 us: per_device(): jnp.einsum('qkgn,nkd->qkgd', weights.astype(jnp.bfloat16), values, prefer...]
    reduce_sum x2 -> x0, other arithmetic: 23.3 us -> none  [the longest x1 21.8 us: per_device(): total_new = jnp.sum(weights, -1)]
    squeeze x2 -> x0, local copies, waits for them, and re-layouts: 6.6 us -> none  [the longest x1 3.93 us: per_device(): old_piece[1]]
    concatenate x1 -> x0, local copies, waits for them, and re-layouts: 5.72 us -> none  [per_device(): jnp.concatenate([jnp.ones((rows, old_piece.shape[1]), bool), pos_piece[0]...]
  transfers between devices with their start and end apart: 4 -> 0, of which waited for: 4 -> 0; matrix products, arithmetic and copies ran while one was open for 20% -> 0% of each run, Pallas kernels for 0% -> 0%
where the time goes in v2:
time: 249 us
  Pallas kernels  242 us (97%)
  other arithmetic  4.2 us (2%)
  local copies, waits for them, and re-layouts  2.92 us (1%)
    pallas_call x1, Pallas kernels, moe(): pl.pallas_call(moe_kernel, out_shape=jax.ShapeDtypeStruct(residual_own.sh...  123 us
    pallas_call x1, Pallas kernels, attention(): pl.pallas_call(attention_kernel, out_shape=(jax.ShapeDtypeStruct((rows, m...  119 us

profile of v2, /device:TPU:1, one launch (start us, length us, event | category | flops | bytes accessed | tf_op | source)
XLA Modules:
  0.0 249.2 jit_solution(16186472449210124279)
XLA Ops:
  0.0 0.8 compare_reduce_fusion
  0.8 0.1 iota_compare_fusion.2
  0.9 0.1 copy.18
  1.0 0.1 fusion
  1.1 0.8 fusion.6
  1.9 0.1 and.131
  2.0 0.1 eq.105
  2.1 0.1 eq.96
  2.2 0.1 broadcast_compare_fusion
  2.3 0.7 bitcast_compare_fusion
  3.0 0.1 copy.17
  3.1 0.1 fusion.4
  3.2 0.1 copy.16
  3.3 0.1 copy.19
  3.4 0.1 and_convert_fusion
  3.6 0.7 copy.22
  4.3 0.7 fusion.3.mix_lo
  5.0 0.7 fusion.2.mix_hi
  5.8 118.9 %attention.1 = (bf16[128,4096]{1,0:T(8,128)(2,1)}, f32[16,4096]{1,0:T(8,128)}) custom-call(bf16[128,1024]{1,0:T(8,128)(2,1)} %query.1, bf16[2,128,512]{2,1,0:T(8,128)(2,1)} %new_kv.1, bf16[2,256,512]{2,1,0:T(8,128)(2,1)} %old_kv.1, s32[1,128]{1,0:T(1,128)} %bitcast.40, bf16[1024,128]{1,0:T(8,128)(2,1)} %o_weight.1, bf16[16,4096]{1,0:T(8,128)(2,1)} %hidden.1, ...), custom_call_target="tpu_custom_call" | custom-call | tf_op jit(solution)/shard_map/attention/pallas_call | solution.py:314
  124.7 122.9 %moe.1 = bf16[16,4096]{1,0:T(8,128)(2,1)} custom-call(bf16[128,4096]{1,0:T(8,128)(2,1)} %get-tuple-element.7.normed, f32[16,4096]{1,0:T(8,128)} %get-tuple-element.8.residual_own, bf16[128,128]{1,0:T(8,128)(2,1)} %get-tuple-element.10.pick, bf16[128,512]{1,0:T(8,128)(2,1)} %bitcast.30, bf16[4,128,256]{2,1,0:T(8,128)(2,1)} %fusion.2.mix_hi, ...), custom_call_target="tpu_custom_call" | custom-call | tf_op jit(solution)/shard_map/moe/pallas_call | solution.py:620
  247.6 1.6 copy.24
  (9 shorter events, 0.1 us)

commit v3 on v2

--- a/solution.py
+++ b/solution.py
@@ -355,16 +355,61 @@
     )(query, new_kv, old_kv, new_pos.reshape(1, rows), o_weight, hidden, norm_gain.reshape(1, model))
 
 
+def tables(ids, gates, pick, pick_rest, mix_hi, mix_lo):
+    hi, y, core, e = place()
+    chosen = ids[...]
+    weights = gates[...]
+    members, factors = [], []
+    for i in range(8):
+        expert = e * 8 + lax.rem(hi + i // 2, 4) * 2 + lax.rem(y // 2 + i, 2)
+        hit = chosen == expert
+        members.append(jnp.max(jnp.where(hit, 1.0, 0.0), 0, keepdims=True))
+        factors.append(jnp.sum(jnp.where(hit, weights, 0.0), 0, keepdims=True))
+    member = jnp.concatenate(members, 0)
+    row = lax.broadcasted_iota(jnp.int32, (128, 128), 0)
+    column = lax.broadcasted_iota(jnp.int32, (128, 128), 1)
+    before = jnp.where(row < column, 1.0, 0.0).astype(jnp.bfloat16)
+    rank = jnp.dot(member.astype(jnp.bfloat16), before, preferred_element_type=jnp.float32)
+    slot = jnp.where(member > 0.5, rank, -1.0)
+    slots = jnp.concatenate([jnp.broadcast_to(slot[i : i + 1], (16, 128)) for i in range(8)], 0)
+    factor = jnp.concatenate([jnp.broadcast_to(f, (16, 128)) for f in factors], 0)
+    r = row & 15
+    for m in range(5):
+        if m < 4:
+            wanted = jnp.where(r >> 2 == m, 16 + (r & 3), -2)
+        else:
+            wanted = r
+        found = slots == wanted.astype(jnp.float32)
+        ones = jnp.where(found, 1.0, 0.0).astype(jnp.bfloat16)
+        mix = jnp.where(found, factor, 0.0).T
+        high = mix.astype(jnp.bfloat16)
+        low = (mix - high.astype(jnp.float32)).astype(jnp.bfloat16)
+        if m < 4:
+            pick_rest[:, m * 128 : (m + 1) * 128] = ones
+            mix_hi[m, :, 128:256] = high
+            mix_lo[m, :, 128:256] = low
+        else:
+            pick[...] = ones
+            for q in range(4):
+                mix_hi[q, :, 0:128] = high
+                mix_lo[q, :, 0:128] = low
+
+
 def moe_kernel(
     normed,
     residual_own,
+    ids,
+    gates,
+    w_in_hbm,
+    w_out_hbm,
+    out_ref,
+    w_in,
+    w_out,
+    w_sem,
     pick,
     pick_rest,
     mix_hi,
     mix_lo,
-    w_in,
-    w_out,
-    out_ref,
     sent,
     got,
     both,
@@ -418,6 +463,14 @@
             barrier, inc=1, device_id=(lax.axis_index("ctx"), other(d)), device_id_type=MESH
         )
 
+    loads = [
+        pltpu.make_async_copy(w_in_hbm, w_in, w_sem.at[0]),
+        pltpu.make_async_copy(w_out_hbm, w_out, w_sem.at[1]),
+    ]
+    for load in loads:
+        load.start()
+    tables(ids, gates, pick, pick_rest, mix_hi, mix_lo)
+
     for m in range(4):
         rows = jnp.dot(
             pick[...], normed[:, m * width : (m + 1) * width], preferred_element_type=jnp.float32
@@ -439,7 +492,7 @@
         None if i == 0 else remote(sent.at[i], got.at[i], d_send.at[i], d_recv.at[i], there(i))
         for i in range(8)
     ]
-    for i in (4, 5, 2, 6, 3, 7, 1):
+    for i in (2, 6, 1):
         d_copy[i].start()
     f_copy = [
         remote(got.at[i], got.at[16 + i], f_send.at[i], f_recv.at[i], pair) for i in range(8)
@@ -453,6 +506,14 @@
     order = (0,) + ARRIVE
     for n in range(8):
         i = order[n]
+        if i == 2:
+            for sent_now, begun in ((2, 3), (6, 7)):
+                d_copy[sent_now].wait_send()
+                d_copy[begun].start()
+        if i == 3:
+            for sent_now, begun in ((3, 4), (7, 5)):
+                d_copy[sent_now].wait_send()
+                d_copy[begun].start()
         if i > 0:
             d_copy[i].wait_recv()
         f_copy[i].start()
@@ -518,6 +579,8 @@
 
     for i in order:
         c_copy[i].wait_recv()
+    for load in loads:
+        load.wait()
     experts(0)
     rc_copy = [
         remote(part.at[8 + i], from_core.at[i], rc_send.at[i], rc_recv.at[i], sibling)
@@ -546,25 +609,30 @@
         for i in range(8)
     ]
     final = (4, 5, 2, 6, 3, 7, 1, 0)
-    for i in final:
-        rc_copy[8 + i].wait_recv()
-        to_pair[i] = (
-            part[16 + i].astype(jnp.float32) + from_core[8 + i].astype(jnp.float32)
-        ).astype(jnp.bfloat16)
-        rf_copy[i].start()
-    for i in final:
-        rc_copy[i].wait_recv()
-        rf_copy[i].wait_recv()
-        total = (
-            part[i].astype(jnp.float32)
-            + from_core[i].astype(jnp.float32)
-            + from_pair[i].astype(jnp.float32)
-        ).astype(jnp.bfloat16)
-        if i == 0:
-            home[0] = total
-        else:
-            to_home[i] = total
-            rd_copy[i].start()
+    for n in range(10):
+        if n < 8:
+            i = final[n]
+            rc_copy[8 + i].wait_recv()
+            to_pair[i] = (
+                part[16 + i].astype(jnp.float32) + from_core[8 + i].astype(jnp.float32)
+            ).astype(jnp.bfloat16)
+            if n >= 2:
+                rf_copy[final[n - 2]].wait_send()
+            rf_copy[i].start()
+        if n >= 2:
+            i = final[n - 2]
+            rc_copy[i].wait_recv()
+            rf_copy[i].wait_recv()
+            total = (
+                part[i].astype(jnp.float32)
+                + from_core[i].astype(jnp.float32)
+                + from_pair[i].astype(jnp.float32)
+            ).astype(jnp.bfloat16)
+            if i == 0:
+                home[0] = total
+            else:
+                to_home[i] = total
+                rd_copy[i].start()
     for i in ARRIVE:
         rd_copy[i].wait_recv()
 
@@ -598,19 +666,21 @@
         total += from_exp[d].astype(jnp.float32)
     out_ref[...] = total.astype(jnp.bfloat16)
 
+    for i in (1, 4, 5):
+        d_copy[i].wait_send()
+    for i in (1, 0):
+        rf_copy[i].wait_send()
     for i in range(8):
         if i > 0:
-            d_copy[i].wait_send()
             rd_copy[i].wait_send()
             x_copy[i].wait_send()
         f_copy[i].wait_send()
-        rf_copy[i].wait_send()
     for i in range(16):
         c_copy[i].wait_send()
         rc_copy[i].wait_send()
 
 
-def moe(normed, residual_own, pick, pick_rest, mix_hi, mix_lo, w_in, w_out):
+def moe(normed, residual_own, expert_ids, gate_weights, w_in, w_out):
     model = normed.shape[1]
     width = model // 4
     block = (5, 16, width)
@@ -620,9 +690,16 @@
     return pl.pallas_call(
         moe_kernel,
         out_shape=jax.ShapeDtypeStruct(residual_own.shape, half),
-        in_specs=[vmem] * 8,
+        in_specs=[vmem] * 4 + [pl.BlockSpec(memory_space=pl.ANY)] * 2,
         out_specs=vmem,
         scratch_shapes=[
+            pltpu.VMEM(w_in.shape, half),
+            pltpu.VMEM(w_out.shape, half),
+            dma((2,)),
+            pltpu.VMEM((128, 128), half),
+            pltpu.VMEM((128, 512), half),
+            pltpu.VMEM((4, 128, 256), half),
+            pltpu.VMEM((4, 128, 256), half),
             pltpu.VMEM((8,) + block, half),
             pltpu.VMEM((32,) + block, half),
             pltpu.VMEM((320, 2 * FFQ), jnp.float32),
@@ -656,40 +733,7 @@
             collective_id=1, has_side_effects=True, vmem_limit_bytes=56 * 2**20
         ),
         name="moe",
-    )(normed, residual_own, pick, pick_rest, mix_hi, mix_lo, w_in, w_out)
-
-
-def tables(expert_ids, gate_weights):
-    hi, y, core, e = place()
-    i = jnp.arange(8, dtype=jnp.int32)
-    local = ((hi + i // 2) % 4) * 2 + ((y // 2) + i) % 2
-    expert = e * 8 + local
-    ids = expert_ids.T
-    hits = ids[None, :, :] == expert[:, None, None]
-    member = jnp.any(hits, 1)
-    gate = jnp.sum(jnp.where(hits, gate_weights.T[None], 0.0), 1)
-    before = jnp.arange(128)[:, None] < jnp.arange(128)[None, :]
-    rank = jnp.dot(
-        member.astype(jnp.bfloat16), before.astype(jnp.bfloat16), preferred_element_type=jnp.float32
-    ).astype(jnp.int32)
-    slot = jnp.where(member, rank, -1)
-    r = jnp.arange(16, dtype=jnp.int32)
-    pick = slot[:, None, :] == r[None, :, None]
-    m = jnp.arange(4, dtype=jnp.int32)
-    rest = (slot[:, None, None, :] == 16 + (r % 4)[None, :, None, None]) & (
-        (r // 4)[None, :, None, None] == m[None, None, :, None]
-    )
-    mix = jnp.where(pick, gate[:, None, :], 0.0).reshape(128, 128).T
-    mix_rest = jnp.where(rest, gate[:, None, None, :], 0.0).reshape(128, 4, 128).transpose(1, 2, 0)
-    mix = jnp.concatenate([jnp.broadcast_to(mix[None], (4, 128, 128)), mix_rest], 2)
-    mix_hi = mix.astype(jnp.bfloat16)
-    mix_lo = (mix - mix_hi.astype(jnp.float32)).astype(jnp.bfloat16)
-    return (
-        pick.reshape(128, 128).astype(jnp.bfloat16),
-        rest.reshape(128, 512).astype(jnp.bfloat16),
-        mix_hi,
-        mix_lo,
-    )
+    )(normed, residual_own, expert_ids.T, gate_weights.T, w_in, w_out)
 
 
 def per_device(
@@ -709,7 +753,7 @@
         query, new_kv, old_kv, new_pos, o_weight, hidden, norm_gain
     )
     return moe(
-        normed, residual_own, *tables(expert_ids, gate_weights), w_in[0, 0], w_out[0, 0]
+        normed, residual_own, expert_ids, gate_weights, w_in[0, 0], w_out[0, 0]
     )
 
 

time: 249 us -> 239 us (0.960)
  Pallas kernels: 242 us -> 236 us
  other arithmetic: 4.2 us -> 0 us
    pallas_call x1, Pallas kernels: 123 us -> 117 us  [moe(): pl.pallas_call(moe_kernel, out_shape=jax.ShapeDtypeStruct(residual_own.sh...]
where the time goes in v3:
time: 239 us; the launch traced here: 238 us
  Pallas kernels  236 us (99%)
    pallas_call x1, Pallas kernels, attention(): pl.pallas_call(attention_kernel, out_shape=(jax.ShapeDtypeStruct((rows, m...  119 us
    pallas_call x1, Pallas kernels, moe(): pl.pallas_call(moe_kernel, out_shape=jax.ShapeDtypeStruct(residual_own.sh...  117 us

profile of v3, /device:TPU:1, one launch (start us, length us, event | category | flops | bytes accessed | tf_op | source)
XLA Modules:
  0.0 237.6 jit_solution(18336964103193728025)
XLA Ops:
  0.0 119.0 %attention.1 = (bf16[128,4096]{1,0:T(8,128)(2,1)}, f32[16,4096]{1,0:T(8,128)}) custom-call(bf16[128,1024]{1,0:T(8,128)(2,1)} %query.1, bf16[2,128,512]{2,1,0:T(8,128)(2,1)} %new_kv.1, bf16[2,256,512]{2,1,0:T(8,128)(2,1)} %old_kv.1, s32[1,128]{1,0:T(1,128)} %bitcast.11, bf16[1024,128]{1,0:T(8,128)(2,1)} %o_weight.1, bf16[16,4096]{1,0:T(8,128)(2,1)} %hidden.1, ...), custom_call_target="tpu_custom_call" | custom-call | tf_op jit(solution)/shard_map/attention/pallas_call | solution.py:314
  119.0 117.1 %moe.1 = bf16[16,4096]{1,0:T(8,128)(2,1)} custom-call(bf16[128,4096]{1,0:T(8,128)(2,1)} %get-tuple-element.7.normed, f32[16,4096]{1,0:T(8,128)} %get-tuple-element.8.residual_own, s32[8,128]{1,0:T(8,128)} %bitcast.9, f32[8,128]{1,0:T(8,128)} %bitcast.10, bf16[4096,768]{1,0:T(8,128)(2,1)} %bitcast.6, bf16[384,4096]{1,0:T(8,128)(2,1)} %bitcast.7), custom_call_target="tpu_custom_call" | custom-call | tf_op jit(solution)/shard_map/moe/pallas_call | solution.py:690
  236.1 1.6 copy.13

commit v4 on v3

--- a/solution.py
+++ b/solution.py
@@ -9,6 +9,37 @@
 FFQ = 384
 MESH = pl.DeviceIdType.MESH
 ARRIVE = (1, 2, 6, 3, 7, 4, 5)
+ORDER = (0, 4, 1, 3, 5, 7, 2, 6)
+
+
+CHUNKS = ((2, 6, 3, 7), (0, 1, 4, 5))
+SCHEDULE = (
+    ("send", 2, 6, 1),
+    ("pass", 0, 1),
+    ("sent", 2),
+    ("send", 3),
+    ("sent", 6),
+    ("send", 7),
+    ("pass", 2, 6),
+    ("core", 0, 1),
+    ("sent", 3),
+    ("send", 4),
+    ("sent", 7),
+    ("send", 5),
+    ("pass", 3, 7),
+    ("core", 2, 6, 3, 7),
+    ("work", 0),
+    ("pass", 4, 5),
+    ("back", 2, 6),
+    ("core", 4, 5),
+    ("home", 2),
+    ("back", 3, 7),
+    ("home", 6),
+    ("work", 1),
+    ("home", 3, 7),
+    ("back", 4, 5, 1, 0),
+    ("home", 4, 5, 1, 0),
+)
 
 
 def place():
@@ -45,6 +76,9 @@
     attended,
     projected,
     from_exp,
+    summed,
+    pieces,
+    gathered,
     own_normed,
     normed,
     kz_send,
@@ -55,12 +89,14 @@
     kc_recv,
     wz_send,
     wz_recv,
-    wy_send,
-    wy_recv,
-    wc_send,
-    wc_recv,
+    ay_send,
+    ay_recv,
+    ac_send,
+    ac_recv,
     x_send,
     x_recv,
+    p_send,
+    p_recv,
     n_send,
     n_recv,
 ):
@@ -74,12 +110,22 @@
     def along(d):
         return (ctx_of(hi + d, y, core), e)
 
+    low = lax.rem(e, 2)
+    outer = (ctx_of(hi + 3 + 2 * low, y, core), e + 1 - 2 * low)
+    inner = (ctx, e + 1 - 2 * low)
+
+    def behind(s):
+        return (ctx_of(hi, lax.rem(y + 4 - s % 4, 4), core if s < 4 else 1 - core), e)
+
     def other(d):
         return lax.rem(e + d, 8)
 
     barrier = pltpu.get_barrier_semaphore()
-    for device in (along(1), along(2), along(3), up, down, sibling):
-        pl.semaphore_signal(barrier, inc=1, device_id=device, device_id_type=MESH)
+    for d in range(1, 4):
+        pl.semaphore_signal(barrier, inc=1, device_id=along(d), device_id_type=MESH)
+    pl.semaphore_signal(barrier, inc=1, device_id=outer, device_id_type=MESH)
+    for s in range(1, 8):
+        pl.semaphore_signal(barrier, inc=1, device_id=behind(s), device_id_type=MESH)
     for d in range(1, 8):
         pl.semaphore_signal(barrier, inc=1, device_id=(ctx, other(d)), device_id_type=MESH)
 
@@ -98,63 +144,66 @@
     )
     weight[0] = o_weight[...]
 
-    pl.semaphore_wait(barrier, 13)
-
-    def gather(blocks, z_send, z_recv, y_send, y_recv, c_send, c_recv):
-        z_copy = [None] + [
-            remote(blocks.at[0], blocks.at[d], z_send.at[d], z_recv.at[d], along(d))
-            for d in range(1, 4)
-        ]
-        y_copy = {}
-        for d in range(4):
-            for dy, device in ((1, up), (3, down)):
-                y_copy[dy, d] = remote(
-                    blocks.at[d],
-                    blocks.at[dy * 4 + d],
-                    y_send.at[dy * 4 + d],
-                    y_recv.at[dy * 4 + d],
-                    device,
-                )
-            source = 4 + d if d % 2 == 0 else 12 + d
-            y_copy[2, d] = remote(
-                blocks.at[source],
-                blocks.at[8 + d],
-                y_send.at[8 + d],
-                y_recv.at[8 + d],
-                up if d % 2 == 0 else down,
+    pl.semaphore_wait(barrier, 18)
+
+    kz = [None] + [
+        remote(kv.at[d * 8 - 8], kv.at[d * 8], kz_send.at[d], kz_recv.at[d], device)
+        for d, device in ((1, outer), (2, inner), (3, outer))
+    ]
+    wz = [None] + [
+        remote(weight.at[0], weight.at[d], wz_send.at[d], wz_recv.at[d], along(d))
+        for d in range(1, 4)
+    ]
+    ky = {}
+    for d in range(4):
+        for dy, device in ((1, up), (3, down)):
+            ky[dy, d] = remote(
+                kv.at[d * 8],
+                kv.at[d * 8 + dy],
+                ky_send.at[d * 4 + dy],
+                ky_recv.at[d * 4 + dy],
+                device,
             )
-        c_copy = [
-            remote(blocks.at[s], blocks.at[16 + s], c_send.at[s], c_recv.at[s], sibling)
-            for s in range(16)
-        ]
-        return z_copy, y_copy, c_copy
-
-    kz, ky, kc = gather(kv, kz_send, kz_recv, ky_send, ky_recv, kc_send, kc_recv)
-    wz, wy, wc = gather(weight, wz_send, wz_recv, wy_send, wy_recv, wc_send, wc_recv)
-
-    def begin_y(y_copy, c_copy, d):
-        y_copy[1, d].start()
-        y_copy[3, d].start()
-        c_copy[d].start()
-
-    def pass_on(y_copy, c_copy, d):
-        y_copy[1, d].wait_recv()
+        ky[2, d] = remote(
+            kv.at[d * 8 + (1 if d % 2 == 0 else 3)],
+            kv.at[d * 8 + 2],
+            ky_send.at[d * 4 + 2],
+            ky_recv.at[d * 4 + 2],
+            up if d % 2 == 0 else down,
+        )
+    kc = {
+        (dy, d): remote(
+            kv.at[d * 8 + dy],
+            kv.at[d * 8 + 4 + dy],
+            kc_send.at[d * 4 + dy],
+            kc_recv.at[d * 4 + dy],
+            sibling,
+        )
+        for d in range(4)
+        for dy in range(4)
+    }
+
+    def begin_y(d):
+        ky[1, d].start()
+        ky[3, d].start()
+        kc[0, d].start()
+
+    def pass_on(d):
+        ky[1, d].wait_recv()
         if d % 2 == 0:
-            y_copy[2, d].start()
-        c_copy[4 + d].start()
-        y_copy[3, d].wait_recv()
+            ky[2, d].start()
+        kc[1, d].start()
+        ky[3, d].wait_recv()
         if d % 2 == 1:
-            y_copy[2, d].start()
-        c_copy[12 + d].start()
-
-    def last(y_copy, c_copy, d):
-        y_copy[2, d].wait_recv()
-        c_copy[8 + d].start()
-
-    near = (0, 1, 3, 2)
-    for d in (1, 3, 2):
-        kz[d].start()
-    begin_y(ky, kc, 0)
+            ky[2, d].start()
+        kc[3, d].start()
+
+    def last(d):
+        ky[2, d].wait_recv()
+        kc[2, d].start()
+
+    kz[1].start()
+    begin_y(0)
 
     for h in range(8):
         part = query[:, h * HD : (h + 1) * HD].astype(jnp.float32).T.astype(jnp.bfloat16)
@@ -163,21 +212,20 @@
     acc[...] = jnp.zeros_like(acc)
     factor = 1.4426950408889634 / HD**0.5
 
-    def attend(group):
-        base = group * 4
+    def attend(blocks):
         for b in range(4):
-            digits = kv[base + b, 768:784].astype(jnp.float32)
+            digits = kv[blocks[b], 768:784].astype(jnp.float32)
             place_of = digits[0:1] * 64.0 + digits[1:2]
             column = jnp.broadcast_to(place_of, (128, 128)).T
             seen = column <= own_pos.astype(jnp.float32)
             bias[b] = jnp.where(seen, 0.0, -1e30)
 
-        @pl.loop(0, 4)
+        @pl.loop(0, 4, unroll=4)
         def _(t):
             part = queries[t]
             pieces = []
             for b in range(4):
-                scores = jnp.dot(kv[base + b, 0:384], part, preferred_element_type=jnp.float32)
+                scores = jnp.dot(kv[blocks[b], 0:384], part, preferred_element_type=jnp.float32)
                 wide = jnp.concatenate([bias[b], bias[b]], 1)
                 pieces += [scores[:256], scores[256:] + wide]
             old_top = top[t, 0:1]
@@ -189,7 +237,7 @@
             )
             values = jnp.concatenate(
                 [
-                    kv[base + b, 384 + 128 * i : 512 + 128 * i]
+                    kv[blocks[b], 384 + 128 * i : 512 + 128 * i]
                     for b in range(4)
                     for i in range(3)
                 ],
@@ -202,79 +250,146 @@
             acc[t] = acc[t] * jnp.exp2((old_top - new_top) * factor) + added
             top[t] = jnp.broadcast_to(new_top, (8, 256))
 
-    for d in (1, 3, 2):
-        kz[d].wait_recv()
-        begin_y(ky, kc, d)
-    for d in (1, 3, 2):
+    def attend_near(d):
+        kc[0, d].wait_recv()
+        attend([d * 8 + b for b in (0, 4, 1, 3)])
+
+    def attend_far(d):
+        for dy in (1, 3, 2):
+            kc[dy, d].wait_recv()
+        attend([d * 8 + b for b in (5, 7, 2, 6)])
+
+    kz[1].wait_recv()
+    kz[2].start()
+    begin_y(1)
+    pass_on(0)
+    attend_near(0)
+    kz[2].wait_recv()
+    kz[3].start()
+    begin_y(2)
+    for d in (1, 3):
         wz[d].start()
-    attend(0)
-    for d in near:
-        pass_on(ky, kc, d)
-    begin_y(wy, wc, 0)
-    for d in near:
-        kc[d].wait_recv()
-    attend(4)
-    for d in (1, 3, 2):
-        wz[d].wait_recv()
-        begin_y(wy, wc, d)
-    attend(1)
-    for d in near:
-        last(ky, kc, d)
-    attend(3)
-    for d in near:
-        pass_on(wy, wc, d)
-    attend(2)
-    for d in near:
-        kc[4 + d].wait_recv()
-    attend(5)
-    for d in near:
-        kc[12 + d].wait_recv()
-    attend(7)
-    for d in near:
-        last(wy, wc, d)
-    for d in near:
-        kc[8 + d].wait_recv()
-    attend(6)
+    last(0)
+    pass_on(1)
+    attend_far(0)
+    attend_near(1)
+    kz[3].wait_recv()
+    begin_y(3)
+    wz[2].start()
+    last(1)
+    pass_on(2)
+    attend_far(1)
+    attend_near(2)
+    last(2)
+    pass_on(3)
+    attend_far(2)
+    attend_near(3)
+    last(3)
+    attend_far(3)
 
     for h in range(8):
         part = slice((h % 2) * 128, (h % 2 + 1) * 128)
         scaled = acc[h // 2, 0:128, part] / acc[h // 2, 128:129, part]
-        attended[:, h * HD : (h + 1) * HD] = scaled.T.astype(jnp.bfloat16)
-    for s in range(16):
-        wc[s].wait_recv()
-
-    def column_of(slot):
-        k, dy, dh = slot // 16, (slot // 4) % 4, slot % 4
-        owner = ctx_of(hi + 4 - dh, lax.rem(y + 4 - dy, 4), lax.rem(core + k, 2))
-        return pl.ds(pl.multiple_of(owner * 128, 128), 128)
-
-    @pl.loop(0, 16)
-    def _(n):
-        both = jnp.concatenate([weight[2 * n], weight[2 * n + 1]], 1)
-        result = jnp.dot(attended[...], both, preferred_element_type=jnp.float32)
-        result = result.astype(jnp.bfloat16)
-        projected[:, column_of(2 * n)] = result[:, :128]
-        projected[:, column_of(2 * n + 1)] = result[:, 128:]
+        attended[0, :, h * HD : (h + 1) * HD] = scaled.T.astype(jnp.bfloat16)
+
+    def half_of(slot, k):
+        return attended.at[slot, pl.ds(k * 64, 64)]
+
+    ay = {
+        1: remote(attended.at[0], attended.at[1], ay_send.at[0], ay_recv.at[0], up),
+        3: remote(attended.at[0], attended.at[3], ay_send.at[1], ay_recv.at[1], down),
+        "up": remote(half_of(1, 0), half_of(2, 0), ay_send.at[2], ay_recv.at[2], up),
+        "down": remote(half_of(3, 1), half_of(2, 1), ay_send.at[3], ay_recv.at[3], down),
+    }
+    ac = [
+        remote(attended.at[s], attended.at[4 + s], ac_send.at[s], ac_recv.at[s], sibling)
+        for s in range(4)
+    ]
+    ay[1].start()
+    ay[3].start()
+    ac[0].start()
+    for d in range(1, 4):
+        wz[d].wait_recv()
+
+    def project(s):
+        for pair in range(2):
+            both = jnp.concatenate([weight[2 * pair], weight[2 * pair + 1]], 1)
+            result = jnp.dot(attended[s], both, preferred_element_type=jnp.float32)
+            projected[:, ORDER.index(s), :, pair * 256 : (pair + 1) * 256] = result.astype(
+                jnp.bfloat16
+            ).reshape(8, 16, 256)
+
+    x_copy = [
+        None
+        if d == 0
+        else remote(
+            projected.at[other(d), pl.ds(half * 4, 4)],
+            from_exp.at[d, pl.ds(half * 4, 4)],
+            x_send.at[half * 8 + d],
+            x_recv.at[half * 8 + d],
+            (ctx, other(d)),
+        )
+        for half in range(2)
+        for d in range(8)
+    ]
+    p_copy = [None] + [
+        remote(summed.at[s], pieces.at[s], p_send.at[s], p_recv.at[s], behind(s))
+        for s in range(1, 8)
+    ]
+
+    project(0)
+    ac[0].wait_recv()
+    project(4)
+    ay[1].wait_recv()
+    ay["up"].start()
+    ac[1].start()
+    ay[3].wait_recv()
+    ay["down"].start()
+    ac[3].start()
+    project(1)
+    project(3)
+    for d in range(1, 8):
+        x_copy[d].start()
+    ac[1].wait_recv()
+    project(5)
+    ac[3].wait_recv()
+    project(7)
+    ay["up"].wait_recv()
+    ay["down"].wait_recv()
+    ac[2].start()
+    project(2)
+    ac[2].wait_recv()
+    project(6)
+    for d in range(1, 8):
+        x_copy[8 + d].start()
+
+    for half in range(2):
+        for d in range(1, 8):
+            x_copy[half * 8 + d].wait_recv()
+        for k in range(half * 4, half * 4 + 4):
+            s = ORDER[k]
+            total = projected[e, k].astype(jnp.float32)
+            for d in range(1, 8):
+                total += from_exp[d, k].astype(jnp.float32)
+            if s == 0:
+                pieces[0] = total
+            else:
+                summed[s] = total
+                p_copy[s].start()
+    for s in ORDER:
+        if s > 0:
+            p_copy[s].wait_recv()
+        sender = lax.rem(y + s % 4, 4) * 2 + (core if s < 4 else 1 - core)
+        for d in range(4):
+            owner = lax.rem(hi + 4 - d, 4) * 8 + sender
+            gathered[:, pl.ds(pl.multiple_of(owner * 128, 128), 128)] = pieces[
+                s, :, d * 128 : (d + 1) * 128
+            ]
 
     def rows_of(index):
         return pl.ds(pl.multiple_of(index * 16, 16), 16)
 
-    x_copy = [None] + [
-        remote(
-            projected.at[rows_of(other(d))],
-            from_exp.at[d],
-            x_send.at[d],
-            x_recv.at[d],
-            (ctx, other(d)),
-        )
-        for d in range(1, 8)
-    ]
-    for d in range(1, 8):
-        x_copy[d].start()
-    residual = hidden[...].astype(jnp.float32) + projected[rows_of(e), :].astype(jnp.float32)
-    for d in range(1, 8):
-        x_copy[d].wait_recv()
-        residual += from_exp[d].astype(jnp.float32)
+    residual = hidden[...].astype(jnp.float32) + gathered[...]
     residual_ref[...] = residual
     mean = jnp.sum(residual * residual, 1, keepdims=True) * (1.0 / model)
     own = (residual * lax.rsqrt(mean + 1e-06) * norm_gain[...]).astype(jnp.bfloat16)
@@ -294,14 +409,17 @@
         kz[d].wait_send()
         wz[d].wait_send()
     for d in range(4):
-        for dy in range(1, 4):
-            ky[dy, d].wait_send()
-            wy[dy, d].wait_send()
-    for s in range(16):
-        kc[s].wait_send()
-        wc[s].wait_send()
+        for dy in range(4):
+            if dy > 0:
+                ky[dy, d].wait_send()
+            kc[dy, d].wait_send()
+        ac[d].wait_send()
+    for copy in ay.values():
+        copy.wait_send()
     for d in range(1, 8):
         x_copy[d].wait_send()
+        x_copy[8 + d].wait_send()
+        p_copy[d].wait_send()
         n_copy[d].wait_send()
 
 
@@ -321,15 +439,18 @@
         out_specs=(vmem, vmem),
         scratch_shapes=[
             pltpu.VMEM((32, 784, HD), half),
-            pltpu.VMEM((32,) + o_weight.shape, half),
+            pltpu.VMEM((4,) + o_weight.shape, half),
             pltpu.VMEM((4, HD, 256), half),
             pltpu.VMEM((4, 128, 128), jnp.float32),
             pltpu.VMEM((4, 8, 256), jnp.float32),
             pltpu.VMEM((4, 144, 256), jnp.float32),
-            pltpu.VMEM(query.shape, half),
-            pltpu.VMEM((rows, model), half),
-            pltpu.VMEM((8, 16, model), half),
-            pltpu.VMEM((16, model), half),
+            pltpu.VMEM((8,) + query.shape, half),
+            pltpu.VMEM((8, 8, 16, 512), half),
+            pltpu.VMEM((8, 8, 16, 512), half),
+            pltpu.VMEM((8, 16, 512), jnp.float32),
+            pltpu.VMEM((8, 16, 512), jnp.float32),
+            pltpu.VMEM(hidden.shape, jnp.float32),
+            pltpu.VMEM(hidden.shape, half),
             pltpu.VMEM((rows, model), half),
             dma((4,)),
             dma((4,)),
@@ -339,8 +460,10 @@
             dma((16,)),
             dma((4,)),
             dma((4,)),
-            dma((16,)),
-            dma((16,)),
+            dma((4,)),
+            dma((4,)),
+            dma((4,)),
+            dma((4,)),
             dma((16,)),
             dma((16,)),
             dma((8,)),
@@ -444,6 +567,10 @@
     sibling = (ctx_of(hi, y, 1 - core), e)
     pair = (ctx_of(hi, y + 1 - 2 * lax.rem(y, 2), core), e)
 
+    def slot(i, group):
+        chunk = int(i in CHUNKS[1])
+        return chunk * 16 + group * 4 + CHUNKS[chunk].index(i)
+
     def there(i):
         return (ctx_of(hi + i // 2, y if i % 2 == 0 else 3 - y, core), e)
 
@@ -484,44 +611,36 @@
             preferred_element_type=jnp.float32,
         )
     sent[:, 4] = rest.astype(jnp.bfloat16).reshape(8, 16, width)
-    got[0] = sent[0]
+    got[slot(0, 0)] = sent[0]
 
     pl.semaphore_wait(barrier, 16)
 
     d_copy = [
-        None if i == 0 else remote(sent.at[i], got.at[i], d_send.at[i], d_recv.at[i], there(i))
+        None if i == 0 else remote(
+            sent.at[i], got.at[slot(i, 0)], d_send.at[i], d_recv.at[i], there(i)
+        )
         for i in range(8)
     ]
-    for i in (2, 6, 1):
-        d_copy[i].start()
     f_copy = [
-        remote(got.at[i], got.at[16 + i], f_send.at[i], f_recv.at[i], pair) for i in range(8)
+        remote(got.at[slot(i, 0)], got.at[slot(i, 2)], f_send.at[i], f_recv.at[i], pair)
+        for i in range(8)
     ]
     c_copy = [
-        remote(got.at[i], got.at[8 + i], c_send.at[i], c_recv.at[i], sibling) for i in range(8)
-    ] + [
-        remote(got.at[16 + i], got.at[24 + i], c_send.at[8 + i], c_recv.at[8 + i], sibling)
+        remote(got.at[slot(i, g)], got.at[slot(i, g + 1)], c_send.at[k], c_recv.at[k], sibling)
+        for k, (g, i) in enumerate((g, i) for g in (0, 2) for i in range(8))
+    ]
+    rc_copy = [
+        remote(part.at[slot(i, g)], from_core.at[k], rc_send.at[k], rc_recv.at[k], sibling)
+        for k, (g, i) in enumerate((g, i) for g in (1, 3) for i in range(8))
+    ]
+    rf_copy = [
+        remote(to_pair.at[i], from_pair.at[i], rf_send.at[i], rf_recv.at[i], pair)
         for i in range(8)
     ]
-    order = (0,) + ARRIVE
-    for n in range(8):
-        i = order[n]
-        if i == 2:
-            for sent_now, begun in ((2, 3), (6, 7)):
-                d_copy[sent_now].wait_send()
-                d_copy[begun].start()
-        if i == 3:
-            for sent_now, begun in ((3, 4), (7, 5)):
-                d_copy[sent_now].wait_send()
-                d_copy[begun].start()
-        if i > 0:
-            d_copy[i].wait_recv()
-        f_copy[i].start()
-        c_copy[i].start()
-        if n >= 2:
-            f_copy[order[n - 2]].wait_recv()
-            c_copy[8 + order[n - 2]].start()
-
+    rd_copy = [
+        None if i == 0 else remote(to_home.at[i], home.at[i], rd_send.at[i], rd_recv.at[i], back(i))
+        for i in range(8)
+    ]
     def regroup(m, rows, columns):
         row = lax.broadcasted_iota(jnp.int32, (rows, columns), 0)
         column = lax.broadcasted_iota(jnp.int32, (rows, columns), 1)
@@ -577,54 +696,42 @@
             )
         part[base : base + 16, 4] = rest_part.astype(jnp.bfloat16).reshape(16, 16, width)
 
-    for i in order:
-        c_copy[i].wait_recv()
-    for load in loads:
-        load.wait()
-    experts(0)
-    rc_copy = [
-        remote(part.at[8 + i], from_core.at[i], rc_send.at[i], rc_recv.at[i], sibling)
-        for i in range(8)
-    ] + [
-        remote(part.at[24 + i], from_core.at[8 + i], rc_send.at[8 + i], rc_recv.at[8 + i], sibling)
-        for i in range(8)
-    ]
-    for i in order:
-        rc_copy[i].start()
-    for n in (6, 7):
-        f_copy[order[n]].wait_recv()
-        c_copy[8 + order[n]].start()
-    for i in order:
-        c_copy[8 + i].wait_recv()
-    experts(16)
-    for i in order:
-        rc_copy[8 + i].start()
-
-    rf_copy = [
-        remote(to_pair.at[i], from_pair.at[i], rf_send.at[i], rf_recv.at[i], pair)
-        for i in range(8)
-    ]
-    rd_copy = [
-        None if i == 0 else remote(to_home.at[i], home.at[i], rd_send.at[i], rd_recv.at[i], back(i))
-        for i in range(8)
-    ]
-    final = (4, 5, 2, 6, 3, 7, 1, 0)
-    for n in range(10):
-        if n < 8:
-            i = final[n]
+    for step, i in ((step, i) for step, *blocks in SCHEDULE for i in blocks):
+        if step == "send":
+            d_copy[i].start()
+        elif step == "sent":
+            d_copy[i].wait_send()
+        elif step == "pass":
+            if i > 0:
+                d_copy[i].wait_recv()
+            f_copy[i].start()
+            c_copy[i].start()
+        elif step == "core":
+            f_copy[i].wait_recv()
+            c_copy[8 + i].start()
+        elif step == "work":
+            if i == 0:
+                for load in loads:
+                    load.wait()
+            for block in CHUNKS[i]:
+                c_copy[block].wait_recv()
+                c_copy[8 + block].wait_recv()
+            experts(i * 16)
+            for block in CHUNKS[i]:
+                rc_copy[8 + block].start()
+            for block in CHUNKS[i]:
+                rc_copy[block].start()
+        elif step == "back":
             rc_copy[8 + i].wait_recv()
             to_pair[i] = (
-                part[16 + i].astype(jnp.float32) + from_core[8 + i].astype(jnp.float32)
+                part[slot(i, 2)].astype(jnp.float32) + from_core[8 + i].astype(jnp.float32)
             ).astype(jnp.bfloat16)
-            if n >= 2:
-                rf_copy[final[n - 2]].wait_send()
             rf_copy[i].start()
-        if n >= 2:
-            i = final[n - 2]
+        elif step == "home":
             rc_copy[i].wait_recv()
             rf_copy[i].wait_recv()
             total = (
-                part[i].astype(jnp.float32)
+                part[slot(i, 0)].astype(jnp.float32)
                 + from_core[i].astype(jnp.float32)
                 + from_pair[i].astype(jnp.float32)
             ).astype(jnp.bfloat16)
@@ -666,14 +773,13 @@
         total += from_exp[d].astype(jnp.float32)
     out_ref[...] = total.astype(jnp.bfloat16)
 
-    for i in (1, 4, 5):
-        d_copy[i].wait_send()
-    for i in (1, 0):
-        rf_copy[i].wait_send()
     for i in range(8):
         if i > 0:
             rd_copy[i].wait_send()
             x_copy[i].wait_send()
+            if not any(step == "sent" and i in blocks for step, *blocks in SCHEDULE):
+                d_copy[i].wait_send()
+        rf_copy[i].wait_send()
         f_copy[i].wait_send()
     for i in range(16):
         c_copy[i].wait_send()

time: 239 us -> 211 us (0.88)
  Pallas kernels: 236 us -> 209 us
    pallas_call x1, Pallas kernels: 119 us -> 101 us  [attention(): pl.pallas_call(attention_kernel, out_shape=(jax.ShapeDtypeStruct((rows, m...]
    pallas_call x1, Pallas kernels: 117 us -> 108 us  [moe(): pl.pallas_call(moe_kernel, out_shape=jax.ShapeDtypeStruct(residual_own.sh...]
where the time goes in v4:
time: 211 us
  Pallas kernels  209 us (99%)
    pallas_call x1, Pallas kernels, moe(): pl.pallas_call(moe_kernel, out_shape=jax.ShapeDtypeStruct(residual_own.sh...  108 us
    pallas_call x1, Pallas kernels, attention(): pl.pallas_call(attention_kernel, out_shape=(jax.ShapeDtypeStruct((rows, m...  101 us

profile of v4, /device:TPU:1, one launch (start us, length us, event | category | flops | bytes accessed | tf_op | source)
XLA Modules:
  0.0 210.8 jit_solution(9506175553995341753)
XLA Ops:
  0.0 101.3 %attention.1 = (bf16[128,4096]{1,0:T(8,128)(2,1)}, f32[16,4096]{1,0:T(8,128)}) custom-call(bf16[128,1024]{1,0:T(8,128)(2,1)} %query.1, bf16[2,128,512]{2,1,0:T(8,128)(2,1)} %new_kv.1, bf16[2,256,512]{2,1,0:T(8,128)(2,1)} %old_kv.1, s32[1,128]{1,0:T(1,128)} %bitcast.11, bf16[1024,128]{1,0:T(8,128)(2,1)} %o_weight.1, bf16[16,4096]{1,0:T(8,128)(2,1)} %hidden.1, ...), custom_call_target="tpu_custom_call" | custom-call | tf_op jit(solution)/shard_map/attention/pallas_call | solution.py:432
  101.3 107.9 %moe.1 = bf16[16,4096]{1,0:T(8,128)(2,1)} custom-call(bf16[128,4096]{1,0:T(8,128)(2,1)} %get-tuple-element.7.normed, f32[16,4096]{1,0:T(8,128)} %get-tuple-element.8.residual_own, s32[8,128]{1,0:T(8,128)} %bitcast.9, f32[8,128]{1,0:T(8,128)} %bitcast.10, bf16[4096,768]{1,0:T(8,128)(2,1)} %bitcast.6, bf16[384,4096]{1,0:T(8,128)(2,1)} %bitcast.7), custom_call_target="tpu_custom_call" | custom-call | tf_op jit(solution)/shard_map/moe/pallas_call | solution.py:796
  209.2 1.6 copy.13

commit v5 on v4

--- a/solution.py
+++ b/solution.py
@@ -9,10 +9,12 @@
 FFQ = 384
 MESH = pl.DeviceIdType.MESH
 ARRIVE = (1, 2, 6, 3, 7, 4, 5)
+ATTENTION = 33
+NORMED = 13
 ORDER = (0, 4, 1, 3, 5, 7, 2, 6)
 
 
-CHUNKS = ((2, 6, 3, 7), (0, 1, 4, 5))
+CHUNKS = ((0, 1), (2, 6), (3, 7), (4,), (5,))
 SCHEDULE = (
     ("send", 2, 6, 1),
     ("pass", 0, 1),
@@ -22,23 +24,30 @@
     ("send", 7),
     ("pass", 2, 6),
     ("core", 0, 1),
-    ("sent", 3),
+    ("work", 0),
+    ("sent", 3, 7),
     ("send", 4),
-    ("sent", 7),
+    ("pass", 3, 7),
+    ("core", 2, 6),
+    ("work", 1),
+    ("sent", 4),
     ("send", 5),
-    ("pass", 3, 7),
-    ("core", 2, 6, 3, 7),
-    ("work", 0),
-    ("pass", 4, 5),
+    ("pass", 4),
     ("back", 2, 6),
-    ("core", 4, 5),
-    ("home", 2),
+    ("core", 3, 7),
+    ("work", 2),
+    ("core", 4),
     ("back", 3, 7),
-    ("home", 6),
-    ("work", 1),
+    ("work", 3),
+    ("pass", 5),
+    ("home", 2, 6),
+    ("back", 4),
+    ("core", 5),
     ("home", 3, 7),
-    ("back", 4, 5, 1, 0),
-    ("home", 4, 5, 1, 0),
+    ("work", 4),
+    ("home", 4),
+    ("back", 5, 1, 0),
+    ("home", 5, 1, 0),
 )
 
 
@@ -49,6 +58,11 @@
 
 def ctx_of(hi, y, core):
     return lax.rem(hi, 4) * 8 + y * 2 + core
+
+
+def across(i):
+    hi, y, core, e = place()
+    return (ctx_of(hi + i // 2, y if i % 2 == 0 else 3 - y, core), e)
 
 
 def remote(src, dst, send, recv, device):
@@ -57,7 +71,7 @@
     )
 
 
-def attention_kernel(
+def attention(
     query,
     new_kv,
     old_kv,
@@ -65,8 +79,7 @@
     o_weight,
     hidden,
     norm_gain,
-    normed_ref,
-    residual_ref,
+    meanwhile,
     kv,
     weight,
     queries,
@@ -81,6 +94,7 @@
     gathered,
     own_normed,
     normed,
+    residual_own,
     kz_send,
     kz_recv,
     ky_send,
@@ -110,9 +124,9 @@
     def along(d):
         return (ctx_of(hi + d, y, core), e)
 
-    low = lax.rem(e, 2)
-    outer = (ctx_of(hi + 3 + 2 * low, y, core), e + 1 - 2 * low)
-    inner = (ctx, e + 1 - 2 * low)
+    parity = lax.rem(e, 2)
+    outer = (ctx_of(hi + 3 + 2 * parity, y, core), e + 1 - 2 * parity)
+    inner = (ctx, e + 1 - 2 * parity)
 
     def behind(s):
         return (ctx_of(hi, lax.rem(y + 4 - s % 4, 4), core if s < 4 else 1 - core), e)
@@ -123,6 +137,9 @@
     barrier = pltpu.get_barrier_semaphore()
     for d in range(1, 4):
         pl.semaphore_signal(barrier, inc=1, device_id=along(d), device_id_type=MESH)
+        pl.semaphore_signal(
+            barrier, inc=1, device_id=across(2 * d + 1), device_id_type=MESH
+        )
     pl.semaphore_signal(barrier, inc=1, device_id=outer, device_id_type=MESH)
     for s in range(1, 8):
         pl.semaphore_signal(barrier, inc=1, device_id=behind(s), device_id_type=MESH)
@@ -144,7 +161,7 @@
     )
     weight[0] = o_weight[...]
 
-    pl.semaphore_wait(barrier, 18)
+    pl.semaphore_wait(barrier, 21)
 
     kz = [None] + [
         remote(kv.at[d * 8 - 8], kv.at[d * 8], kz_send.at[d], kz_recv.at[d], device)
@@ -204,6 +221,7 @@
 
     kz[1].start()
     begin_y(0)
+    meanwhile()
 
     for h in range(8):
         part = query[:, h * HD : (h + 1) * HD].astype(jnp.float32).T.astype(jnp.bfloat16)
@@ -390,7 +408,7 @@
         return pl.ds(pl.multiple_of(index * 16, 16), 16)
 
     residual = hidden[...].astype(jnp.float32) + gathered[...]
-    residual_ref[...] = residual
+    residual_own[...] = residual
     mean = jnp.sum(residual * residual, 1, keepdims=True) * (1.0 / model)
     own = (residual * lax.rsqrt(mean + 1e-06) * norm_gain[...]).astype(jnp.bfloat16)
     own_normed[...] = own
@@ -403,7 +421,6 @@
     normed[rows_of(e), :] = own
     for d in range(1, 8):
         n_copy[d].wait_recv()
-    normed_ref[...] = normed[...]
 
     for d in range(1, 4):
         kz[d].wait_send()
@@ -421,61 +438,6 @@
         x_copy[8 + d].wait_send()
         p_copy[d].wait_send()
         n_copy[d].wait_send()
-
-
-def attention(query, new_kv, old_kv, new_pos, o_weight, hidden, norm_gain):
-    rows = query.shape[0]
-    model = hidden.shape[1]
-    half = jnp.bfloat16
-    vmem = pl.BlockSpec(memory_space=pltpu.VMEM)
-    dma = pltpu.SemaphoreType.DMA
-    return pl.pallas_call(
-        attention_kernel,
-        out_shape=(
-            jax.ShapeDtypeStruct((rows, model), half),
-            jax.ShapeDtypeStruct(hidden.shape, jnp.float32),
-        ),
-        in_specs=[vmem] * 7,
-        out_specs=(vmem, vmem),
-        scratch_shapes=[
-            pltpu.VMEM((32, 784, HD), half),
-            pltpu.VMEM((4,) + o_weight.shape, half),
-            pltpu.VMEM((4, HD, 256), half),
-            pltpu.VMEM((4, 128, 128), jnp.float32),
-            pltpu.VMEM((4, 8, 256), jnp.float32),
-            pltpu.VMEM((4, 144, 256), jnp.float32),
-            pltpu.VMEM((8,) + query.shape, half),
-            pltpu.VMEM((8, 8, 16, 512), half),
-            pltpu.VMEM((8, 8, 16, 512), half),
-            pltpu.VMEM((8, 16, 512), jnp.float32),
-            pltpu.VMEM((8, 16, 512), jnp.float32),
-            pltpu.VMEM(hidden.shape, jnp.float32),
-            pltpu.VMEM(hidden.shape, half),
-            pltpu.VMEM((rows, model), half),
-            dma((4,)),
-            dma((4,)),
-            dma((16,)),
-            dma((16,)),
-            dma((16,)),
-            dma((16,)),
-            dma((4,)),
-            dma((4,)),
-            dma((4,)),
-            dma((4,)),
-            dma((4,)),
-            dma((4,)),
-            dma((16,)),
-            dma((16,)),
-            dma((8,)),
-            dma((8,)),
-            dma((8,)),
-            dma((8,)),
-        ],
-        compiler_params=pltpu.CompilerParams(
-            collective_id=2, has_side_effects=True, vmem_limit_bytes=56 * 2**20
-        ),
-        name="attention",
-    )(query, new_kv, old_kv, new_pos.reshape(1, rows), o_weight, hidden, norm_gain.reshape(1, model))
 
 
 def tables(ids, gates, pick, pick_rest, mix_hi, mix_lo):
@@ -518,17 +480,13 @@
                 mix_lo[q, :, 0:128] = low
 
 
-def moe_kernel(
+def moe(
     normed,
     residual_own,
-    ids,
-    gates,
-    w_in_hbm,
-    w_out_hbm,
     out_ref,
+    loads,
     w_in,
     w_out,
-    w_sem,
     pick,
     pick_rest,
     mix_hi,
@@ -568,35 +526,15 @@
     pair = (ctx_of(hi, y + 1 - 2 * lax.rem(y, 2), core), e)
 
     def slot(i, group):
-        chunk = int(i in CHUNKS[1])
-        return chunk * 16 + group * 4 + CHUNKS[chunk].index(i)
-
-    def there(i):
-        return (ctx_of(hi + i // 2, y if i % 2 == 0 else 3 - y, core), e)
+        chunk = [i in blocks for blocks in CHUNKS].index(True)
+        blocks = CHUNKS[chunk]
+        return 4 * sum(map(len, CHUNKS[:chunk])) + group * len(blocks) + blocks.index(i)
 
     def back(i):
         return (ctx_of(hi + 4 - i // 2, y if i % 2 == 0 else 3 - y, core), e)
 
     def other(d):
         return lax.rem(e + d, 8)
-
-    barrier = pltpu.get_barrier_semaphore()
-    for i in range(1, 8):
-        pl.semaphore_signal(barrier, inc=1, device_id=there(i), device_id_type=MESH)
-    pl.semaphore_signal(barrier, inc=1, device_id=sibling, device_id_type=MESH)
-    pl.semaphore_signal(barrier, inc=1, device_id=pair, device_id_type=MESH)
-    for d in range(1, 8):
-        pl.semaphore_signal(
-            barrier, inc=1, device_id=(lax.axis_index("ctx"), other(d)), device_id_type=MESH
-        )
-
-    loads = [
-        pltpu.make_async_copy(w_in_hbm, w_in, w_sem.at[0]),
-        pltpu.make_async_copy(w_out_hbm, w_out, w_sem.at[1]),
-    ]
-    for load in loads:
-        load.start()
-    tables(ids, gates, pick, pick_rest, mix_hi, mix_lo)
 
     for m in range(4):
         rows = jnp.dot(
@@ -613,11 +551,9 @@
     sent[:, 4] = rest.astype(jnp.bfloat16).reshape(8, 16, width)
     got[slot(0, 0)] = sent[0]
 
-    pl.semaphore_wait(barrier, 16)
-
     d_copy = [
         None if i == 0 else remote(
-            sent.at[i], got.at[slot(i, 0)], d_send.at[i], d_recv.at[i], there(i)
+            sent.at[i], got.at[slot(i, 0)], d_send.at[i], d_recv.at[i], across(i)
         )
         for i in range(8)
     ]
@@ -647,22 +583,23 @@
         small, large = (row, column) if rows < columns else (column, row)
         return (large == (small // 4) * 16 + m * 4 + small % 4).astype(jnp.bfloat16)
 
-    def experts(base):
-        rest_rows = got[base : base + 16, 4].reshape(256, width)
+    def experts(base, count):
+        tall, low = count * 16, count * 4
+        rest_rows = got[base : base + count, 4].reshape(tall, width)
         for m in range(4):
-            rest_in[:, m * width : (m + 1) * width] = jnp.dot(
-                regroup(m, 64, 256), rest_rows, preferred_element_type=jnp.float32
+            rest_in[:low, m * width : (m + 1) * width] = jnp.dot(
+                regroup(m, low, tall), rest_rows, preferred_element_type=jnp.float32
             ).astype(jnp.bfloat16)
 
         @pl.loop(0, 3)
         def _(n):
             columns = pl.ds(pl.multiple_of(n * 256, 256), 256)
-            total = jnp.zeros((320, 256), jnp.float32)
+            total = jnp.zeros((tall + low, 256), jnp.float32)
             for m in range(4):
                 rows = jnp.concatenate(
                     [
-                        got[base : base + 16, m].reshape(256, width),
-                        rest_in[:, m * width : (m + 1) * width],
+                        got[base : base + count, m].reshape(tall, width),
+                        rest_in[:low, m * width : (m + 1) * width],
                     ],
                     0,
                 )
@@ -671,10 +608,12 @@
                     w_in[m * width : (m + 1) * width, columns],
                     preferred_element_type=jnp.float32,
                 )
-            both[:, columns] = total
-
-        gate = both[:, :FFQ]
-        act[...] = (gate / (1.0 + jnp.exp(-gate)) * both[:, FFQ:]).astype(jnp.bfloat16)
+            both[: tall + low, columns] = total
+
+        gate = both[: tall + low, :FFQ]
+        act[: tall + low] = (gate / (1.0 + jnp.exp(-gate)) * both[: tall + low, FFQ:]).astype(
+            jnp.bfloat16
+        )
         steps = width // 256
 
         @pl.loop(0, 4 * steps)
@@ -682,20 +621,21 @@
             columns = pl.ds(pl.multiple_of(n * 256, 256), 256)
             inner = pl.ds(pl.multiple_of((n % steps) * 256, 256), 256)
             result = jnp.dot(
-                act[...], w_out[:, columns], preferred_element_type=jnp.float32
+                act[: tall + low], w_out[:, columns], preferred_element_type=jnp.float32
             ).astype(jnp.bfloat16)
-            part[base : base + 16, n // steps, :, inner] = result[:256].reshape(16, 16, 256)
-            rest_out[:, columns] = result[256:]
-
-        rest_part = jnp.zeros((256, width), jnp.float32)
+            part[base : base + count, n // steps, :, inner] = result[:tall].reshape(count, 16, 256)
+            rest_out[:low, columns] = result[tall:]
+
+        rest_part = jnp.zeros((tall, width), jnp.float32)
         for m in range(4):
             rest_part += jnp.dot(
-                regroup(m, 256, 64),
-                rest_out[:, m * width : (m + 1) * width],
+                regroup(m, tall, low),
+                rest_out[:low, m * width : (m + 1) * width],
                 preferred_element_type=jnp.float32,
             )
-        part[base : base + 16, 4] = rest_part.astype(jnp.bfloat16).reshape(16, 16, width)
-
+        part[base : base + count, 4] = rest_part.astype(jnp.bfloat16).reshape(count, 16, width)
+
+    loaded = False
     for step, i in ((step, i) for step, *blocks in SCHEDULE for i in blocks):
         if step == "send":
             d_copy[i].start()
@@ -710,13 +650,14 @@
             f_copy[i].wait_recv()
             c_copy[8 + i].start()
         elif step == "work":
-            if i == 0:
+            if not loaded:
                 for load in loads:
                     load.wait()
+                loaded = True
             for block in CHUNKS[i]:
                 c_copy[block].wait_recv()
                 c_copy[8 + block].wait_recv()
-            experts(i * 16)
+            experts(slot(CHUNKS[i][0], 0), 4 * len(CHUNKS[i]))
             for block in CHUNKS[i]:
                 rc_copy[8 + block].start()
             for block in CHUNKS[i]:
@@ -786,60 +727,112 @@
         rc_copy[i].wait_send()
 
 
-def moe(normed, residual_own, expert_ids, gate_weights, w_in, w_out):
-    model = normed.shape[1]
+def kernel(*refs):
+    inputs, (ids, gates, w_in_hbm, w_out_hbm, out_ref), rest = refs[:7], refs[7:12], refs[12:]
+    first, (w_in, w_out, w_sem), second = rest[:ATTENTION], rest[ATTENTION:][:3], rest[ATTENTION:][3:]
+    loads = [
+        pltpu.make_async_copy(w_in_hbm, w_in, w_sem.at[0]),
+        pltpu.make_async_copy(w_out_hbm, w_out, w_sem.at[1]),
+    ]
+
+    def meanwhile():
+        for load in loads:
+            load.start()
+        tables(ids, gates, *second[:4])
+
+    attention(*inputs, meanwhile, *first)
+    moe(first[NORMED], first[NORMED + 1], out_ref, loads, w_in, w_out, *second)
+
+
+def layer(
+    query,
+    new_kv,
+    old_kv,
+    new_pos,
+    o_weight,
+    hidden,
+    norm_gain,
+    expert_ids,
+    gate_weights,
+    w_in,
+    w_out,
+):
+    rows = query.shape[0]
+    model = hidden.shape[1]
     width = model // 4
     block = (5, 16, width)
     half = jnp.bfloat16
     vmem = pl.BlockSpec(memory_space=pltpu.VMEM)
-    dma = pltpu.SemaphoreType.DMA
+
+    def dma(*counts):
+        return [pltpu.SemaphoreType.DMA((count,)) for count in counts for _ in range(2)]
+
+    first = [
+        pltpu.VMEM((32, 784, HD), half),
+        pltpu.VMEM((4,) + o_weight.shape, half),
+        pltpu.VMEM((4, HD, 256), half),
+        pltpu.VMEM((4, 128, 128), jnp.float32),
+        pltpu.VMEM((4, 8, 256), jnp.float32),
+        pltpu.VMEM((4, 144, 256), jnp.float32),
+        pltpu.VMEM((8,) + query.shape, half),
+        pltpu.VMEM((8, 8, 16, 512), half),
+        pltpu.VMEM((8, 8, 16, 512), half),
+        pltpu.VMEM((8, 16, 512), jnp.float32),
+        pltpu.VMEM((8, 16, 512), jnp.float32),
+        pltpu.VMEM(hidden.shape, jnp.float32),
+        pltpu.VMEM(hidden.shape, half),
+        pltpu.VMEM((rows, model), half),
+        pltpu.VMEM(hidden.shape, jnp.float32),
+    ] + dma(4, 16, 16, 4, 4, 4, 16, 8, 8)
+    assert len(first) == ATTENTION
+    loaded = [
+        pltpu.VMEM(w_in.shape, half),
+        pltpu.VMEM(w_out.shape, half),
+        pltpu.SemaphoreType.DMA((2,)),
+    ]
+    second = [
+        pltpu.VMEM((128, 128), half),
+        pltpu.VMEM((128, 512), half),
+        pltpu.VMEM((4, 128, 256), half),
+        pltpu.VMEM((4, 128, 256), half),
+        pltpu.VMEM((8,) + block, half),
+        pltpu.VMEM((32,) + block, half),
+        pltpu.VMEM((160, 2 * FFQ), jnp.float32),
+        pltpu.VMEM((32, model), half),
+        pltpu.VMEM((160, FFQ), half),
+        pltpu.VMEM((32, model), half),
+        pltpu.VMEM((32,) + block, half),
+        pltpu.VMEM((16,) + block, half),
+        pltpu.VMEM((8,) + block, half),
+        pltpu.VMEM((8,) + block, half),
+        pltpu.VMEM((8,) + block, half),
+        pltpu.VMEM((8,) + block, half),
+        pltpu.VMEM((128, model), half),
+        pltpu.VMEM((8, 16, model), half),
+    ] + dma(8, 8, 16, 16, 8, 8, 8)
     return pl.pallas_call(
-        moe_kernel,
-        out_shape=jax.ShapeDtypeStruct(residual_own.shape, half),
-        in_specs=[vmem] * 4 + [pl.BlockSpec(memory_space=pl.ANY)] * 2,
+        kernel,
+        out_shape=jax.ShapeDtypeStruct(hidden.shape, half),
+        in_specs=[vmem] * 9 + [pl.BlockSpec(memory_space=pl.ANY)] * 2,
         out_specs=vmem,
-        scratch_shapes=[
-            pltpu.VMEM(w_in.shape, half),
-            pltpu.VMEM(w_out.shape, half),
-            dma((2,)),
-            pltpu.VMEM((128, 128), half),
-            pltpu.VMEM((128, 512), half),
-            pltpu.VMEM((4, 128, 256), half),
-            pltpu.VMEM((4, 128, 256), half),
-            pltpu.VMEM((8,) + block, half),
-            pltpu.VMEM((32,) + block, half),
-            pltpu.VMEM((320, 2 * FFQ), jnp.float32),
-            pltpu.VMEM((64, model), half),
-            pltpu.VMEM((320, FFQ), half),
-            pltpu.VMEM((64, model), half),
-            pltpu.VMEM((32,) + block, half),
-            pltpu.VMEM((16,) + block, half),
-            pltpu.VMEM((8,) + block, half),
-            pltpu.VMEM((8,) + block, half),
-            pltpu.VMEM((8,) + block, half),
-            pltpu.VMEM((8,) + block, half),
-            pltpu.VMEM((128, model), half),
-            pltpu.VMEM((8, 16, model), half),
-            dma((8,)),
-            dma((8,)),
-            dma((8,)),
-            dma((8,)),
-            dma((16,)),
-            dma((16,)),
-            dma((16,)),
-            dma((16,)),
-            dma((8,)),
-            dma((8,)),
-            dma((8,)),
-            dma((8,)),
-            dma((8,)),
-            dma((8,)),
-        ],
+        scratch_shapes=first + loaded + second,
         compiler_params=pltpu.CompilerParams(
-            collective_id=1, has_side_effects=True, vmem_limit_bytes=56 * 2**20
+            collective_id=1, has_side_effects=True, vmem_limit_bytes=58 * 2**20
         ),
-        name="moe",
-    )(normed, residual_own, expert_ids.T, gate_weights.T, w_in, w_out)
+        name="layer",
+    )(
+        query,
+        new_kv,
+        old_kv,
+        new_pos.reshape(1, rows),
+        o_weight,
+        hidden,
+        norm_gain.reshape(1, model),
+        expert_ids.T,
+        gate_weights.T,
+        w_in,
+        w_out,
+    )
 
 
 def per_device(
@@ -855,11 +848,18 @@
     w_in,
     w_out,
 ):
-    normed, residual_own = attention(
-        query, new_kv, old_kv, new_pos, o_weight, hidden, norm_gain
-    )
-    return moe(
-        normed, residual_own, expert_ids, gate_weights, w_in[0, 0], w_out[0, 0]
+    return layer(
+        query,
+        new_kv,
+        old_kv,
+        new_pos,
+        o_weight,
+        hidden,
+        norm_gain,
+        expert_ids,
+        gate_weights,
+        w_in[0, 0],
+        w_out[0, 0],
     )
 
 

time: 211 us -> 197 us (0.934); the launches traced: 211 us -> 195 us
  Pallas kernels: 209 us -> 193 us
    pallas_call x2 -> x1, Pallas kernels: 209 us -> 193 us  [layer(): pl.pallas_call(kernel, out_shape=jax.ShapeDtypeStruct(hidden.shape, half)...]
where the time goes in v5:
time: 197 us; the launch traced here: 195 us
  Pallas kernels  193 us (98%)
    pallas_call x1, Pallas kernels, layer(): pl.pallas_call(kernel, out_shape=jax.ShapeDtypeStruct(hidden.shape, half)...  193 us

profile of v5, /device:TPU:1, one launch (start us, length us, event | category | flops | bytes accessed | tf_op | source)
XLA Modules:
  0.0 194.7 jit_solution(5702615272616614477)
XLA Ops:
  0.0 193.1 %layer.1 = bf16[16,4096]{1,0:T(8,128)(2,1)} custom-call(bf16[128,1024]{1,0:T(8,128)(2,1)} %refs_0_.1, bf16[2,128,512]{2,1,0:T(8,128)(2,1)} %refs_1_.1, bf16[2,256,512]{2,1,0:T(8,128)(2,1)} %refs_2_.1, s32[1,128]{1,0:T(1,128)} %bitcast.11, bf16[1024,128]{1,0:T(8,128)(2,1)} %refs_4_.1, bf16[16,4096]{1,0:T(8,128)(2,1)} %refs_5_.1, f32[1,4096]{1,0:T(1,128)} %bitcast.8, ...), custom_call_target="tpu_custom_call" | custom-call | tf_op jit(solution)/shard_map/layer/pallas_call | solution.py:813
  193.1 1.6 copy.13

commit v6 on v5

--- a/solution.py
+++ b/solution.py
@@ -181,13 +181,15 @@
                 ky_recv.at[d * 4 + dy],
                 device,
             )
-        ky[2, d] = remote(
-            kv.at[d * 8 + (1 if d % 2 == 0 else 3)],
-            kv.at[d * 8 + 2],
-            ky_send.at[d * 4 + 2],
-            ky_recv.at[d * 4 + 2],
-            up if d % 2 == 0 else down,
-        )
+        for part, dy, device in ((0, 1, up), (1, 3, down)):
+            some = pl.ds(400 * part, 400 - 16 * part)
+            ky["up" if part == 0 else "down", d] = remote(
+                kv.at[d * 8 + dy, some],
+                kv.at[d * 8 + 2, some],
+                ky_send.at[d * 4 + 2 * part],
+                ky_recv.at[d * 4 + 2 * part],
+                device,
+            )
     kc = {
         (dy, d): remote(
             kv.at[d * 8 + dy],
@@ -207,16 +209,15 @@
 
     def pass_on(d):
         ky[1, d].wait_recv()
-        if d % 2 == 0:
-            ky[2, d].start()
+        ky["up", d].start()
         kc[1, d].start()
         ky[3, d].wait_recv()
-        if d % 2 == 1:
-            ky[2, d].start()
+        ky["down", d].start()
         kc[3, d].start()
 
     def last(d):
-        ky[2, d].wait_recv()
+        ky["up", d].wait_recv()
+        ky["down", d].wait_recv()
         kc[2, d].start()
 
     kz[1].start()
@@ -290,10 +291,10 @@
     last(0)
     pass_on(1)
     attend_far(0)
-    attend_near(1)
     kz[3].wait_recv()
     begin_y(3)
     wz[2].start()
+    attend_near(1)
     last(1)
     pass_on(2)
     attend_far(1)
@@ -427,9 +428,9 @@
         wz[d].wait_send()
     for d in range(4):
         for dy in range(4):
-            if dy > 0:
-                ky[dy, d].wait_send()
             kc[dy, d].wait_send()
+        for step in (1, 3, "up", "down"):
+            ky[step, d].wait_send()
         ac[d].wait_send()
     for copy in ay.values():
         copy.wait_send()
@@ -684,40 +685,40 @@
     for i in ARRIVE:
         rd_copy[i].wait_recv()
 
+    own = pl.ds(pl.multiple_of(e * 16, 16), 16)
+    x_copy = []
     for m in range(4):
         rows = jnp.concatenate(
             [home[:, m].reshape(128, width), home[:, 4].reshape(128, width)], 0
         )
-        mixed[:, m * width : (m + 1) * width] = (
+        mixed[m] = (
             jnp.dot(mix_hi[m], rows, preferred_element_type=jnp.float32)
             + jnp.dot(mix_lo[m], rows, preferred_element_type=jnp.float32)
         ).astype(jnp.bfloat16)
-
-    x_copy = [None]
-    for d in range(1, 8):
-        own = pl.ds(pl.multiple_of(other(d) * 16, 16), 16)
-        x_copy.append(
-            remote(
-                mixed.at[own],
-                from_exp.at[d],
-                x_send.at[d],
-                x_recv.at[d],
+        for d in range(1, 8):
+            theirs = pl.ds(pl.multiple_of(other(d) * 16, 16), 16)
+            copy = remote(
+                mixed.at[m, theirs],
+                from_exp.at[d, m],
+                x_send.at[m * 8 + d],
+                x_recv.at[m * 8 + d],
                 (lax.axis_index("ctx"), other(d)),
             )
-        )
-        x_copy[d].start()
-    total = (
-        residual_own[...] + mixed[pl.ds(pl.multiple_of(e * 16, 16), 16), :].astype(jnp.float32)
-    )
-    for d in range(1, 8):
-        x_copy[d].wait_recv()
-        total += from_exp[d].astype(jnp.float32)
-    out_ref[...] = total.astype(jnp.bfloat16)
-
+            copy.start()
+            x_copy.append(copy)
+    for m in range(4):
+        columns = slice(m * width, (m + 1) * width)
+        total = residual_own[:, columns] + mixed[m, own, :].astype(jnp.float32)
+        for d in range(1, 8):
+            x_copy[m * 7 + d - 1].wait_recv()
+            total += from_exp[d, m].astype(jnp.float32)
+        out_ref[:, columns] = total.astype(jnp.bfloat16)
+
+    for copy in x_copy:
+        copy.wait_send()
     for i in range(8):
         if i > 0:
             rd_copy[i].wait_send()
-            x_copy[i].wait_send()
             if not any(step == "sent" and i in blocks for step, *blocks in SCHEDULE):
                 d_copy[i].wait_send()
         rf_copy[i].wait_send()
@@ -807,9 +808,9 @@
         pltpu.VMEM((8,) + block, half),
         pltpu.VMEM((8,) + block, half),
         pltpu.VMEM((8,) + block, half),
-        pltpu.VMEM((128, model), half),
-        pltpu.VMEM((8, 16, model), half),
-    ] + dma(8, 8, 16, 16, 8, 8, 8)
+        pltpu.VMEM((4, 128, width), half),
+        pltpu.VMEM((8, 4, 16, width), half),
+    ] + dma(8, 8, 16, 16, 8, 8, 32)
     return pl.pallas_call(
         kernel,
         out_shape=jax.ShapeDtypeStruct(hidden.shape, half),

time: 197 us -> 195 us (0.990); the launches traced: 195 us -> 195 us
  no operation moved by 1% of the time
where the time goes in v6:
time: 195 us
  Pallas kernels  193 us (99%)
    pallas_call x1, Pallas kernels, layer(): pl.pallas_call(kernel, out_shape=jax.ShapeDtypeStruct(hidden.shape, half)...  193 us

profile of v6, /device:TPU:1, one launch (start us, length us, event | category | flops | bytes accessed | tf_op | source)
XLA Modules:
  0.0 194.8 jit_solution(12500139930785962885)
XLA Ops:
  0.0 193.2 %layer.1 = bf16[16,4096]{1,0:T(8,128)(2,1)} custom-call(bf16[128,1024]{1,0:T(8,128)(2,1)} %refs_0_.1, bf16[2,128,512]{2,1,0:T(8,128)(2,1)} %refs_1_.1, bf16[2,256,512]{2,1,0:T(8,128)(2,1)} %refs_2_.1, s32[1,128]{1,0:T(1,128)} %bitcast.11, bf16[1024,128]{1,0:T(8,128)(2,1)} %refs_4_.1, bf16[16,4096]{1,0:T(8,128)(2,1)} %refs_5_.1, f32[1,4096]{1,0:T(1,128)} %bitcast.8, ...), custom_call_target="tpu_custom_call" | custom-call | tf_op jit(solution)/shard_map/layer/pallas_call | solution.py:814
  193.2 1.6 copy.13

commit v7 on v6

--- a/solution.py
+++ b/solution.py
@@ -232,7 +232,7 @@
     factor = 1.4426950408889634 / HD**0.5
 
     def attend(blocks):
-        for b in range(4):
+        for b in range(len(blocks)):
             digits = kv[blocks[b], 768:784].astype(jnp.float32)
             place_of = digits[0:1] * 64.0 + digits[1:2]
             column = jnp.broadcast_to(place_of, (128, 128)).T
@@ -243,7 +243,7 @@
         def _(t):
             part = queries[t]
             pieces = []
-            for b in range(4):
+            for b in range(len(blocks)):
                 scores = jnp.dot(kv[blocks[b], 0:384], part, preferred_element_type=jnp.float32)
                 wide = jnp.concatenate([bias[b], bias[b]], 1)
                 pieces += [scores[:256], scores[256:] + wide]
@@ -257,7 +257,7 @@
             values = jnp.concatenate(
                 [
                     kv[blocks[b], 384 + 128 * i : 512 + 128 * i]
-                    for b in range(4)
+                    for b in range(len(blocks))
                     for i in range(3)
                 ],
                 1,
@@ -304,7 +304,11 @@
     attend_far(2)
     attend_near(3)
     last(3)
-    attend_far(3)
+    kc[1, 3].wait_recv()
+    kc[3, 3].wait_recv()
+    attend([29, 31])
+    kc[2, 3].wait_recv()
+    attend([26, 30])
 
     for h in range(8):
         part = slice((h % 2) * 128, (h % 2 + 1) * 128)
@@ -342,15 +346,20 @@
         None
         if d == 0
         else remote(
-            projected.at[other(d), pl.ds(half * 4, 4)],
-            from_exp.at[d, pl.ds(half * 4, 4)],
-            x_send.at[half * 8 + d],
-            x_recv.at[half * 8 + d],
+            projected.at[other(d), pl.ds(pair * 2, 2)],
+            from_exp.at[d, pl.ds(pair * 2, 2)],
+            x_send.at[pair * 8 + d],
+            x_recv.at[pair * 8 + d],
             (ctx, other(d)),
         )
-        for half in range(2)
+        for pair in range(4)
         for d in range(8)
     ]
+
+    def begin_x(pair):
+        for d in range(1, 8):
+            x_copy[pair * 8 + d].start()
+
     p_copy = [None] + [
         remote(summed.at[s], pieces.at[s], p_send.at[s], p_recv.at[s], behind(s))
         for s in range(1, 8)
@@ -359,6 +368,7 @@
     project(0)
     ac[0].wait_recv()
     project(4)
+    begin_x(0)
     ay[1].wait_recv()
     ay["up"].start()
     ac[1].start()
@@ -367,25 +377,24 @@
     ac[3].start()
     project(1)
     project(3)
-    for d in range(1, 8):
-        x_copy[d].start()
+    begin_x(1)
     ac[1].wait_recv()
     project(5)
     ac[3].wait_recv()
     project(7)
+    begin_x(2)
     ay["up"].wait_recv()
     ay["down"].wait_recv()
     ac[2].start()
     project(2)
     ac[2].wait_recv()
     project(6)
-    for d in range(1, 8):
-        x_copy[8 + d].start()
-
-    for half in range(2):
+    begin_x(3)
+
+    for pair in range(4):
         for d in range(1, 8):
-            x_copy[half * 8 + d].wait_recv()
-        for k in range(half * 4, half * 4 + 4):
+            x_copy[pair * 8 + d].wait_recv()
+        for k in range(pair * 2, pair * 2 + 2):
             s = ORDER[k]
             total = projected[e, k].astype(jnp.float32)
             for d in range(1, 8):
@@ -435,8 +444,8 @@
     for copy in ay.values():
         copy.wait_send()
     for d in range(1, 8):
-        x_copy[d].wait_send()
-        x_copy[8 + d].wait_send()
+        for pair in range(4):
+            x_copy[pair * 8 + d].wait_send()
         p_copy[d].wait_send()
         n_copy[d].wait_send()
 
@@ -784,7 +793,7 @@
         pltpu.VMEM(hidden.shape, half),
         pltpu.VMEM((rows, model), half),
         pltpu.VMEM(hidden.shape, jnp.float32),
-    ] + dma(4, 16, 16, 4, 4, 4, 16, 8, 8)
+    ] + dma(4, 16, 16, 4, 4, 4, 32, 8, 8)
     assert len(first) == ATTENTION
     loaded = [
         pltpu.VMEM(w_in.shape, half),

time: 195 us -> 191 us (0.979)
  Pallas kernels: 193 us -> 189 us
    pallas_call x1, Pallas kernels: 193 us -> 189 us  [layer(): pl.pallas_call(kernel, out_shape=jax.ShapeDtypeStruct(hidden.shape, half)...]
where the time goes in v7:
time: 191 us
  Pallas kernels  189 us (99%)
    pallas_call x1, Pallas kernels, layer(): pl.pallas_call(kernel, out_shape=jax.ShapeDtypeStruct(hidden.shape, half)...  189 us

profile of v7, /device:TPU:1, one launch (start us, length us, event | category | flops | bytes accessed | tf_op | source)
XLA Modules:
  0.0 190.7 jit_solution(11972045572041389408)
XLA Ops:
  0.0 189.1 %layer.1 = bf16[16,4096]{1,0:T(8,128)(2,1)} custom-call(bf16[128,1024]{1,0:T(8,128)(2,1)} %refs_0_.1, bf16[2,128,512]{2,1,0:T(8,128)(2,1)} %refs_1_.1, bf16[2,256,512]{2,1,0:T(8,128)(2,1)} %refs_2_.1, s32[1,128]{1,0:T(1,128)} %bitcast.11, bf16[1024,128]{1,0:T(8,128)(2,1)} %refs_4_.1, bf16[16,4096]{1,0:T(8,128)(2,1)} %refs_5_.1, f32[1,4096]{1,0:T(1,128)} %bitcast.8, ...), custom_call_target="tpu_custom_call" | custom-call | tf_op jit(solution)/shard_map/layer/pallas_call | solution.py:823
  189.1 1.6 copy.13

commit v8 on v7

--- a/solution.py
+++ b/solution.py
@@ -159,7 +159,6 @@
         .astype(jnp.float32)
         .astype(jnp.bfloat16)
     )
-    weight[0] = o_weight[...]
 
     pl.semaphore_wait(barrier, 21)
 
@@ -222,6 +221,7 @@
 
     kz[1].start()
     begin_y(0)
+    weight[0] = o_weight[...]
     meanwhile()
 
     for h in range(8):
@@ -269,46 +269,40 @@
             acc[t] = acc[t] * jnp.exp2((old_top - new_top) * factor) + added
             top[t] = jnp.broadcast_to(new_top, (8, 256))
 
-    def attend_near(d):
-        kc[0, d].wait_recv()
-        attend([d * 8 + b for b in (0, 4, 1, 3)])
-
-    def attend_far(d):
-        for dy in (1, 3, 2):
+    def attend_from(blocks, *handed):
+        for dy, d in handed:
             kc[dy, d].wait_recv()
-        attend([d * 8 + b for b in (5, 7, 2, 6)])
-
+        attend(blocks)
+
+    attend_from([0, 4], (0, 0))
     kz[1].wait_recv()
     kz[2].start()
     begin_y(1)
     pass_on(0)
-    attend_near(0)
+    attend_from([1, 3, 5, 7], (1, 0), (3, 0))
     kz[2].wait_recv()
     kz[3].start()
     begin_y(2)
     for d in (1, 3):
         wz[d].start()
     last(0)
+    attend_from([8, 12], (0, 1))
     pass_on(1)
-    attend_far(0)
+    attend_from([2, 6, 9, 11], (2, 0))
     kz[3].wait_recv()
     begin_y(3)
     wz[2].start()
-    attend_near(1)
+    attend_from([13, 15, 16, 20], (1, 1), (3, 1), (0, 2))
     last(1)
     pass_on(2)
-    attend_far(1)
-    attend_near(2)
+    attend_from([10, 14, 17, 19], (2, 1))
+    attend_from([21, 23, 24, 28], (1, 2), (3, 2), (0, 3))
     last(2)
     pass_on(3)
-    attend_far(2)
-    attend_near(3)
+    attend_from([18, 22, 25, 27], (2, 2))
     last(3)
-    kc[1, 3].wait_recv()
-    kc[3, 3].wait_recv()
-    attend([29, 31])
-    kc[2, 3].wait_recv()
-    attend([26, 30])
+    attend_from([29, 31], (1, 3), (3, 3))
+    attend_from([26, 30], (2, 3))
 
     for h in range(8):
         part = slice((h % 2) * 128, (h % 2 + 1) * 128)

time: 191 us -> 190 us (level)
  Pallas kernels: 189 us -> 187 us
    pallas_call x1, Pallas kernels: 189 us -> 187 us  [layer(): pl.pallas_call(kernel, out_shape=jax.ShapeDtypeStruct(hidden.shape, half)...]
where the time goes in v8:
time: 190 us; the launch traced here: 189 us
  Pallas kernels  187 us (98%)
    pallas_call x1, Pallas kernels, layer(): pl.pallas_call(kernel, out_shape=jax.ShapeDtypeStruct(hidden.shape, half)...  187 us

profile of v8, /device:TPU:1, one launch (start us, length us, event | category | flops | bytes accessed | tf_op | source)
XLA Modules:
  0.0 188.6 jit_solution(1178695132898342949)
XLA Ops:
  0.0 187.0 %layer.1 = bf16[16,4096]{1,0:T(8,128)(2,1)} custom-call(bf16[128,1024]{1,0:T(8,128)(2,1)} %refs_0_.1, bf16[2,128,512]{2,1,0:T(8,128)(2,1)} %refs_1_.1, bf16[2,256,512]{2,1,0:T(8,128)(2,1)} %refs_2_.1, s32[1,128]{1,0:T(1,128)} %bitcast.11, bf16[1024,128]{1,0:T(8,128)(2,1)} %refs_4_.1, bf16[16,4096]{1,0:T(8,128)(2,1)} %refs_5_.1, f32[1,4096]{1,0:T(1,128)} %bitcast.8, ...), custom_call_target="tpu_custom_call" | custom-call | tf_op jit(solution)/shard_map/layer/pallas_call | solution.py:817
  187.0 1.6 copy.13

commit v9 on v8

--- a/solution.py
+++ b/solution.py
@@ -283,15 +283,14 @@
     kz[2].wait_recv()
     kz[3].start()
     begin_y(2)
-    for d in (1, 3):
-        wz[d].start()
     last(0)
     attend_from([8, 12], (0, 1))
     pass_on(1)
     attend_from([2, 6, 9, 11], (2, 0))
     kz[3].wait_recv()
     begin_y(3)
-    wz[2].start()
+    for d in (1, 3, 2):
+        wz[d].start()
     attend_from([13, 15, 16, 20], (1, 1), (3, 1), (0, 2))
     last(1)
     pass_on(2)

time: 190 us -> 186 us (0.979)
  Pallas kernels: 187 us -> 185 us
    pallas_call x1, Pallas kernels: 187 us -> 185 us  [layer(): pl.pallas_call(kernel, out_shape=jax.ShapeDtypeStruct(hidden.shape, half)...]
where the time goes in v9:
time: 186 us
  Pallas kernels  185 us (99%)
    pallas_call x1, Pallas kernels, layer(): pl.pallas_call(kernel, out_shape=jax.ShapeDtypeStruct(hidden.shape, half)...  185 us

profile of v9, /device:TPU:1, one launch (start us, length us, event | category | flops | bytes accessed | tf_op | source)
XLA Modules:
  0.0 186.3 jit_solution(4098071249405622012)
XLA Ops:
  0.0 184.7 %layer.1 = bf16[16,4096]{1,0:T(8,128)(2,1)} custom-call(bf16[128,1024]{1,0:T(8,128)(2,1)} %refs_0_.1, bf16[2,128,512]{2,1,0:T(8,128)(2,1)} %refs_1_.1, bf16[2,256,512]{2,1,0:T(8,128)(2,1)} %refs_2_.1, s32[1,128]{1,0:T(1,128)} %bitcast.11, bf16[1024,128]{1,0:T(8,128)(2,1)} %refs_4_.1, bf16[16,4096]{1,0:T(8,128)(2,1)} %refs_5_.1, f32[1,4096]{1,0:T(1,128)} %bitcast.8, ...), custom_call_target="tpu_custom_call" | custom-call | tf_op jit(solution)/shard_map/layer/pallas_call | solution.py:816
  184.7 1.6 copy.13
